TPU v7x, 32 devices: a whole 2x2x4 slice. The times are simulated.
32 devices in a mesh: tp: 2 (over x), cp: 16 (over z, y, core).
Axes of the slice: x: 2, y: 2, z: 4, core: 2. Of those that a mesh axis runs over, the one named last changes fastest.
Arguments:
- signal: bfloat16 [2048, 4096], P('cp', 'tp'), may hold values from -6 to 6
- cotangent: bfloat16 [2048, 4096], P('cp', 'tp'), may hold values from -0.125 to 0.125
- long_filter: bfloat16 [2048, 2048], P('cp'), may hold values from -6 to 6
Outputs:
- grad_signal: bfloat16 [2048, 4096], P('cp', 'tp')
- grad_filter: bfloat16 [2048, 2048], P('cp')
All inputs are finite; a program needn't handle non-finite values.
Results may differ from a plain program's by a relative error of at most 0.0015.
Values may be sent and summed in bfloat16 or wider, within the bound.
No kernel may reach another device: no remote copies, remote signals or barrier semaphores. Data moves between devices by JAX's collectives and lax.ppermute only.
A program may use at most 128 MiB of HBM per device.

v0:
```python
import math

import jax
import jax.numpy as jnp
from jax import lax
from jax.sharding import PartitionSpec as P

highest = lax.Precision.HIGHEST
full_turn = 2.0 * math.pi


def phases(rows, cols, length, sign, row_start, col_start):
    row_ids = row_start + lax.broadcasted_iota(jnp.int32, (rows, cols), 0)
    col_ids = col_start + lax.broadcasted_iota(jnp.int32, (rows, cols), 1)
    angle = (row_ids * col_ids % length).astype(jnp.float32) * (full_turn / length)
    return (jnp.cos(angle), sign * jnp.sin(angle))


def product(left_real, left_imag, right_real, right_imag):
    return (
        left_real * right_real - left_imag * right_imag,
        left_real * right_imag + left_imag * right_real,
    )


def apply_table(form, table_real, table_imag, data_real, data_imag):
    real = jnp.einsum(form, table_real, data_real, precision=highest) - jnp.einsum(
        form, table_imag, data_imag, precision=highest
    )
    imag = jnp.einsum(form, table_imag, data_real, precision=highest) + jnp.einsum(
        form, table_real, data_imag, precision=highest
    )
    return (real, imag)


def transform_rows(data_real, data_imag, sign):
    total = data_real.shape[0]
    trailing = data_real.shape[1:]
    inner = max((factor for factor in range(1, math.isqrt(total) + 1) if total % factor == 0))
    outer = total // inner
    part_real = data_real.reshape(outer, inner, -1)
    part_imag = data_imag.reshape(outer, inner, -1)
    table_real, table_imag = phases(outer, outer, outer, sign, 0, 0)
    part_real, part_imag = apply_table("qk,qpr->kpr", table_real, table_imag, part_real, part_imag)
    twist_real, twist_imag = phases(outer, inner, total, sign, 0, 0)
    part_real, part_imag = product(
        part_real, part_imag, twist_real[:, :, None], twist_imag[:, :, None]
    )
    table_real, table_imag = phases(inner, inner, inner, sign, 0, 0)
    part_real, part_imag = apply_table("pm,kpr->mkr", table_real, table_imag, part_real, part_imag)
    return (part_real.reshape((total,) + trailing), part_imag.reshape((total,) + trailing))


def transform_blocks(source, row_start, total):
    count = source.shape[0]
    span = source.shape[1]
    table_real, table_imag = phases(count, 2 * count, 2 * count, -1.0, 0, 0)
    part_real = jnp.einsum("ac,abr->bcr", table_real, source, precision=highest)
    part_imag = jnp.einsum("ac,abr->bcr", table_imag, source, precision=highest)
    twist_real, twist_imag = phases(span, 2 * count, total, -1.0, row_start, 0)
    return product(part_real, part_imag, twist_real[:, :, None], twist_imag[:, :, None])


def collect_blocks(part_real, part_imag, count, total):
    table_real, table_imag = phases(count, 2 * count, 2 * count, 1.0, 0, 0)
    real = jnp.einsum("ac,bcr->abr", table_real, part_real, precision=highest)
    real = real - jnp.einsum("ac,bcr->abr", table_imag, part_imag, precision=highest)
    return real * (1.0 / total)


def body(signal, cotangent, long_filter):
    positions, columns = signal.shape
    devices = lax.axis_size("cp")
    place = lax.axis_index("cp")
    total = 2 * positions * devices
    slab = positions // devices
    shaped = (
        signal.reshape(1, positions, columns),
        cotangent.reshape(1, positions, columns),
        long_filter.reshape(1, positions, columns),
    )
    moved = (
        lax.all_to_all(shaped[0], "cp", split_axis=1, concat_axis=0, tiled=True),
        lax.all_to_all(shaped[1], "cp", split_axis=1, concat_axis=0, tiled=True),
        lax.all_to_all(shaped[2], "cp", split_axis=1, concat_axis=0, tiled=True),
    )
    halves = [transform_blocks(piece.astype(jnp.float32), place * slab, total) for piece in moved]
    spectra = (
        lax.all_to_all(halves[0][0], "cp", split_axis=1, concat_axis=0, tiled=True),
        lax.all_to_all(halves[0][1], "cp", split_axis=1, concat_axis=0, tiled=True),
        lax.all_to_all(halves[1][0], "cp", split_axis=1, concat_axis=0, tiled=True),
        lax.all_to_all(halves[1][1], "cp", split_axis=1, concat_axis=0, tiled=True),
        lax.all_to_all(halves[2][0], "cp", split_axis=1, concat_axis=0, tiled=True),
        lax.all_to_all(halves[2][1], "cp", split_axis=1, concat_axis=0, tiled=True),
    )
    sig_real, sig_imag = transform_rows(spectra[0], spectra[1], -1.0)
    cot_real, cot_imag = transform_rows(spectra[2], spectra[3], -1.0)
    fil_real, fil_imag = transform_rows(spectra[4], spectra[5], -1.0)
    first_real = fil_real * cot_real + fil_imag * cot_imag
    first_imag = fil_real * cot_imag - fil_imag * cot_real
    second_real = sig_real * cot_real + sig_imag * cot_imag
    second_imag = sig_real * cot_imag - sig_imag * cot_real
    second_real, second_imag = lax.psum((second_real, second_imag), "tp")
    col_start = 2 * place
    inverted = []
    for pair_real, pair_imag in ((first_real, first_imag), (second_real, second_imag)):
        part_real, part_imag = transform_rows(pair_real, pair_imag, 1.0)
        twist_real, twist_imag = phases(positions, part_real.shape[1], total, 1.0, 0, col_start)
        inverted.append(
            product(part_real, part_imag, twist_real[:, :, None], twist_imag[:, :, None])
        )
    returned = (
        lax.all_to_all(inverted[0][0], "cp", split_axis=0, concat_axis=1, tiled=True),
        lax.all_to_all(inverted[0][1], "cp", split_axis=0, concat_axis=1, tiled=True),
        lax.all_to_all(inverted[1][0], "cp", split_axis=0, concat_axis=1, tiled=True),
        lax.all_to_all(inverted[1][1], "cp", split_axis=0, concat_axis=1, tiled=True),
    )
    grad_sig = collect_blocks(returned[0], returned[1], devices, total)
    grad_fil = collect_blocks(returned[2], returned[3], devices, total)
    results = (
        lax.all_to_all(
            grad_sig.astype(jnp.bfloat16), "cp", split_axis=0, concat_axis=1, tiled=True
        ),
        lax.all_to_all(
            grad_fil.astype(jnp.bfloat16), "cp", split_axis=0, concat_axis=1, tiled=True
        ),
    )
    return (results[0].reshape(positions, columns), results[1].reshape(positions, columns))


def solution(mesh):
    in_specs = (P("cp", "tp"), P("cp", "tp"), P("cp", None))
    out_specs = (P("cp", "tp"), P("cp", None))
    return jax.shard_map(body, mesh=mesh, in_specs=in_specs, out_specs=out_specs, check_vma=False)
```

profile of v0, /device:TPU:0, one launch (start us, length us, event | category | flops | bytes accessed | tf_op | source)
XLA Modules:
  0.0 950.8 jit_solution(4428661788175644239)
XLA Ops:
  14.6 7.4 all-to-all-start.3
  27.9 8.5 all-to-all-done.3
  36.5 16.0 %all-to-all-start = ((bf16[16,2,8192]{2,1,0:T(2,128)(2,1)}), bf16[16,2,8192]{2,1,0:T(2,128)(2,1)S(1)}, u32[]{:S(2)}, u32[]{:S(2)}) async-start(bf16[16,2,8192]{2,1,0:T(2,128)(2,1)} %reshape.252), calls=%async_computation | async-start | bytes 1048576 | tf_op jit(solution)/shard_map/all_to_all | solution.py:85
  59.4 7.6 all-to-all-done
  90.1 7.0 multiply_add_fusion.4
  107.9 37.0 %all-to-all-done.4 = f32[8,32,2048]{2,0,1:T(8,128)S(1)} async-done(((f32[8,32,2048]{2,0,1:T(8,128)}), f32[8,32,2048]{2,0,1:T(8,128)S(1)}, u32[]{:S(2)}, u32[]{:S(2)}) %all-to-all-start.4) | async-done | bytes 2097184 | tf_op jit(solution)/shard_map/all_to_all | solution.py:91
  144.9 11.7 %all-to-all-start.5 = ((f32[8,32,2048]{2,0,1:T(8,128)}), f32[8,32,2048]{2,0,1:T(8,128)}, u32[]{:S(2)}, u32[]{:S(2)}) async-start(f32[8,32,2048]{2,0,1:T(8,128)} %copy.216), calls=%async_computation.5 | async-start | bytes 4194304 | tf_op jit(solution)/shard_map/all_to_all | solution.py:92
  160.8 37.0 %all-to-all-done.5 = f32[8,32,2048]{2,0,1:T(8,128)} async-done(((f32[8,32,2048]{2,0,1:T(8,128)}), f32[8,32,2048]{2,0,1:T(8,128)}, u32[]{:S(2)}, u32[]{:S(2)}) %all-to-all-start.5) | async-done | bytes 2097184 | tf_op jit(solution)/shard_map/all_to_all | solution.py:92
  197.8 11.3 %all-to-all-start.1 = ((f32[8,32,2048]{2,0,1:T(8,128)}), f32[8,32,2048]{2,0,1:T(8,128)}, u32[]{:S(2)}, u32[]{:S(2)}) async-start(f32[8,32,2048]{2,0,1:T(8,128)} %copy.205), calls=%async_computation.1 | async-start | bytes 4194304 | tf_op jit(solution)/shard_map/all_to_all | solution.py:93
  213.1 37.0 %all-to-all-done.1 = f32[8,32,2048]{2,0,1:T(8,128)} async-done(((f32[8,32,2048]{2,0,1:T(8,128)}), f32[8,32,2048]{2,0,1:T(8,128)}, u32[]{:S(2)}, u32[]{:S(2)}) %all-to-all-start.1) | async-done | bytes 2097184 | tf_op jit(solution)/shard_map/all_to_all | solution.py:93
  250.2 11.3 %all-to-all-start.2 = ((f32[8,32,2048]{2,0,1:T(8,128)}), f32[8,32,2048]{2,0,1:T(8,128)}, u32[]{:S(2)}, u32[]{:S(2)}) async-start(f32[8,32,2048]{2,0,1:T(8,128)} %copy.207), calls=%async_computation.2 | async-start | bytes 4194304 | tf_op jit(solution)/shard_map/all_to_all | solution.py:94
  265.6 37.0 %all-to-all-done.2 = f32[8,32,2048]{2,0,1:T(8,128)} async-done(((f32[8,32,2048]{2,0,1:T(8,128)}), f32[8,32,2048]{2,0,1:T(8,128)}, u32[]{:S(2)}, u32[]{:S(2)}) %all-to-all-start.2) | async-done | bytes 2097184 | tf_op jit(solution)/shard_map/all_to_all | solution.py:94
  302.6 11.3 %all-to-all-start.10 = ((f32[8,32,2048]{2,0,1:T(8,128)}), f32[8,32,2048]{2,0,1:T(8,128)}, u32[]{:S(2)}, u32[]{:S(2)}) async-start(f32[8,32,2048]{2,0,1:T(8,128)} %copy.246), calls=%async_computation.10 | async-start | bytes 4194304 | tf_op jit(solution)/shard_map/all_to_all | solution.py:89
  318.0 37.0 %all-to-all-done.10 = f32[8,32,2048]{2,0,1:T(8,128)} async-done(((f32[8,32,2048]{2,0,1:T(8,128)}), f32[8,32,2048]{2,0,1:T(8,128)}, u32[]{:S(2)}, u32[]{:S(2)}) %all-to-all-start.10) | async-done | bytes 2097184 | tf_op jit(solution)/shard_map/all_to_all | solution.py:89
  355.0 11.3 %all-to-all-start.11 = ((f32[8,32,2048]{2,0,1:T(8,128)}), f32[8,32,2048]{2,0,1:T(8,128)}, u32[]{:S(2)}, u32[]{:S(2)}) async-start(f32[8,32,2048]{2,0,1:T(8,128)} %copy.248), calls=%async_computation.11 | async-start | bytes 4194304 | tf_op jit(solution)/shard_map/all_to_all | solution.py:90
  381.1 4.5 copy.361
  437.0 4.6 copy.354
  448.4 5.7 multiply_add_fusion.3
  486.5 5.5 multiply_subtract_fusion.2
  518.6 90.7 %all-reduce.3.cloned.1.call-done = (f32[16,8,4096]{2,0,1:T(8,128)}, f32[16,8,4096]{2,0,1:T(8,128)}) async-done(((f32[16,8,4096]{2,0,1:T(8,128)}, f32[16,8,4096]{2,0,1:T(8,128)}), (f32[16,8,4096]{2,0,1:T(8,128)}, f32[16,8,4096]{2,0,1:T(8,128)})) %all-reduce.3.cloned.1.call-update) | async-done | bytes 4194320 | tf_op jit(solution)/shard_map/psum | solution.py:103
  627.6 4.7 fusion.8
  646.2 5.2 convolution_add_fusion.4
  658.0 4.6 convolution_subtract_fusion
  678.0 7.8 multiply_add_fusion
  685.7 52.8 %all_to_all.216 = f32[128,2,2048]{2,1,0:T(2,128)} all-to-all(f32[128,2,2048]{2,1,0:T(2,128)S(1)} %get-tuple-element.9), channel_id=1, replica_groups=mesh['tp'=2,'cp'=16] {'cp'}, dimensions={0} | all-to-all | bytes 4194304 | tf_op jit(solution)/shard_map/all_to_all | solution.py:115
  738.6 52.2 %all_to_all.217 = f32[128,2,2048]{2,1,0:T(2,128)S(1)} all-to-all(f32[128,2,2048]{2,1,0:T(2,128)S(1)} %get-tuple-element.8), channel_id=1, replica_groups=mesh['tp'=2,'cp'=16] {'cp'}, dimensions={0} | all-to-all | bytes 4194304 | tf_op jit(solution)/shard_map/all_to_all | solution.py:116
  790.8 52.3 %all_to_all.218 = f32[128,2,2048]{2,1,0:T(2,128)} all-to-all(f32[128,2,2048]{2,1,0:T(2,128)S(1)} %get-tuple-element.30), channel_id=1, replica_groups=mesh['tp'=2,'cp'=16] {'cp'}, dimensions={0} | all-to-all | bytes 4194304 | tf_op jit(solution)/shard_map/all_to_all | solution.py:113
  843.1 5.6 all-to-all-start.7
  870.2 19.6 %all-to-all-done.7 = f32[128,2,2048]{2,1,0:T(2,128)} async-done(((f32[128,2,2048]{2,1,0:T(2,128)}), f32[128,2,2048]{2,1,0:T(2,128)}, u32[]{:S(2)}, u32[]{:S(2)}) %all-to-all-start.7) | async-done | bytes 2097184 | tf_op jit(solution)/shard_map/all_to_all | solution.py:114
  889.8 11.4 %all-to-all-start.14 = ((bf16[16,8,2048]{2,1,0:T(8,128)(2,1)}), bf16[16,8,2048]{2,1,0:T(8,128)(2,1)S(1)}, u32[]{:S(2)}, u32[]{:S(2)}) async-start(bf16[16,8,2048]{2,1,0:T(8,128)(2,1)} %copy.268), calls=%async_computation.14 | async-start | bytes 1048576 | tf_op jit(solution)/shard_map/all_to_all | solution.py:124
  921.6 6.1 all-to-all-start.8
  927.8 14.5 %all-to-all-done.8 = bf16[16,8,2048]{2,1,0:T(8,128)(2,1)S(1)} async-done(((bf16[16,8,2048]{2,1,0:T(8,128)(2,1)}), bf16[16,8,2048]{2,1,0:T(8,128)(2,1)S(1)}, u32[]{:S(2)}, u32[]{:S(2)}) %all-to-all-start.8) | async-done | bytes 524320 | tf_op jit(solution)/shard_map/all_to_all | solution.py:121
  (153 shorter events, 299.9 us)
Async XLA Ops:
  9.0 13.0 %copy-start.14 = (bf16[128,2048]{1,0:T(8,128)(2,1)S(1)}, bf16[128,2048]{1,0:T(8,128)(2,1)}, u32[]{:S(2)}) copy-start(bf16[128,2048]{1,0:T(8,128)(2,1)} %param.5) | copy-start | bytes 1572868
  14.6 21.9 %all-to-all-start.3 = ((bf16[16,2,8192]{2,1,0:T(2,128)(2,1)}), bf16[16,2,8192]{2,1,0:T(2,128)(2,1)S(1)}, u32[]{:S(2)}, u32[]{:S(2)}) async-start(bf16[16,2,8192]{2,1,0:T(2,128)(2,1)} %reshape.254), calls=%async_computation.3 | async-start | bytes 1048576 | tf_op jit(solution)/shard_map/all_to_all | solution.py:84
  22.8 29.7 %copy-start.15 = (bf16[128,2048]{1,0:T(8,128)(2,1)S(1)}, bf16[128,2048]{1,0:T(8,128)(2,1)}, u32[]{:S(2)}) copy-start(bf16[128,2048]{1,0:T(8,128)(2,1)} %param.3) | copy-start | bytes 1572868
  36.5 30.5 %all-to-all-start = ((bf16[16,2,8192]{2,1,0:T(2,128)(2,1)}), bf16[16,2,8192]{2,1,0:T(2,128)(2,1)S(1)}, u32[]{:S(2)}, u32[]{:S(2)}) async-start(bf16[16,2,8192]{2,1,0:T(2,128)(2,1)} %reshape.252), calls=%async_computation | async-start | bytes 1048576 | tf_op jit(solution)/shard_map/all_to_all | solution.py:85
  67.0 18.7 %all-to-all-start.9 = ((bf16[16,2,8192]{2,1,0:T(2,128)(2,1)}), bf16[16,2,8192]{2,1,0:T(2,128)(2,1)}, u32[]{:S(2)}, u32[]{:S(2)}) async-start(bf16[16,2,8192]{2,1,0:T(2,128)(2,1)} %reshape.256), calls=%async_computation.9 | async-start | bytes 1048576 | tf_op jit(solution)/shard_map/all_to_all | solution.py:83
  87.9 1.7 copy-start.12
  87.9 2.2 copy-start.13
  99.7 45.2 %all-to-all-start.4 = ((f32[8,32,2048]{2,0,1:T(8,128)}), f32[8,32,2048]{2,0,1:T(8,128)S(1)}, u32[]{:S(2)}, u32[]{:S(2)}) async-start(f32[8,32,2048]{2,0,1:T(8,128)} %copy.214), calls=%async_computation.4 | async-start | bytes 4194304 | tf_op jit(solution)/shard_map/all_to_all | solution.py:91
  144.9 52.8 %all-to-all-start.5 = ((f32[8,32,2048]{2,0,1:T(8,128)}), f32[8,32,2048]{2,0,1:T(8,128)}, u32[]{:S(2)}, u32[]{:S(2)}) async-start(f32[8,32,2048]{2,0,1:T(8,128)} %copy.216), calls=%async_computation.5 | async-start | bytes 4194304 | tf_op jit(solution)/shard_map/all_to_all | solution.py:92
  197.8 52.4 %all-to-all-start.1 = ((f32[8,32,2048]{2,0,1:T(8,128)}), f32[8,32,2048]{2,0,1:T(8,128)}, u32[]{:S(2)}, u32[]{:S(2)}) async-start(f32[8,32,2048]{2,0,1:T(8,128)} %copy.205), calls=%async_computation.1 | async-start | bytes 4194304 | tf_op jit(solution)/shard_map/all_to_all | solution.py:93
  250.2 52.4 %all-to-all-start.2 = ((f32[8,32,2048]{2,0,1:T(8,128)}), f32[8,32,2048]{2,0,1:T(8,128)}, u32[]{:S(2)}, u32[]{:S(2)}) async-start(f32[8,32,2048]{2,0,1:T(8,128)} %copy.207), calls=%async_computation.2 | async-start | bytes 4194304 | tf_op jit(solution)/shard_map/all_to_all | solution.py:94
  302.6 52.4 %all-to-all-start.10 = ((f32[8,32,2048]{2,0,1:T(8,128)}), f32[8,32,2048]{2,0,1:T(8,128)}, u32[]{:S(2)}, u32[]{:S(2)}) async-start(f32[8,32,2048]{2,0,1:T(8,128)} %copy.246), calls=%async_computation.10 | async-start | bytes 4194304 | tf_op jit(solution)/shard_map/all_to_all | solution.py:89
  355.0 82.0 %all-to-all-start.11 = ((f32[8,32,2048]{2,0,1:T(8,128)}), f32[8,32,2048]{2,0,1:T(8,128)}, u32[]{:S(2)}, u32[]{:S(2)}) async-start(f32[8,32,2048]{2,0,1:T(8,128)} %copy.248), calls=%async_computation.11 | async-start | bytes 4194304 | tf_op jit(solution)/shard_map/all_to_all | solution.py:90
  366.3 243.0 %all-reduce.3.cloned.1.call-start = ((), (), s32[]{:S(2)}) async-start(), calls=%async_computation.15 | async-start | bytes 8388608 | tf_op jit(solution)/shard_map/psum | solution.py:103
  407.2 3.7 copy-start.2
  410.9 1.9 copy-start.3
  414.8 1.9 copy-start.4
  426.9 3.3 copy-start.1
  444.7 3.7 copy-start.6
  444.7 3.7 copy-start.7
  444.7 3.7 copy-start.8
  609.4 3.7 copy-start.11
  613.0 1.9 copy-start.5
  615.0 2.2 copy-start.9
  615.0 2.2 copy-start.10
  620.4 16.0 %copy-start = (f32[16,8,4096]{2,0,1:T(8,128)}, f32[16,8,4096]{2,0,1:T(8,128)S(1)}, u32[]{:S(2)}) copy-start(f32[16,8,4096]{2,0,1:T(8,128)S(1)} %get-tuple-element.33) | copy-start | bytes 6291460
  843.1 46.7 %all-to-all-start.7 = ((f32[128,2,2048]{2,1,0:T(2,128)}), f32[128,2,2048]{2,1,0:T(2,128)}, u32[]{:S(2)}, u32[]{:S(2)}) async-start(f32[128,2,2048]{2,1,0:T(2,128)} %get-tuple-element.31), calls=%async_computation.7 | async-start | bytes 4194304 | tf_op jit(solution)/shard_map/all_to_all | solution.py:114
  889.8 31.8 %all-to-all-start.14 = ((bf16[16,8,2048]{2,1,0:T(8,128)(2,1)}), bf16[16,8,2048]{2,1,0:T(8,128)(2,1)S(1)}, u32[]{:S(2)}, u32[]{:S(2)}) async-start(bf16[16,8,2048]{2,1,0:T(8,128)(2,1)} %copy.268), calls=%async_computation.14 | async-start | bytes 1048576 | tf_op jit(solution)/shard_map/all_to_all | solution.py:124
  921.6 20.6 %all-to-all-start.8 = ((bf16[16,8,2048]{2,1,0:T(8,128)(2,1)}), bf16[16,8,2048]{2,1,0:T(8,128)(2,1)S(1)}, u32[]{:S(2)}, u32[]{:S(2)}) async-start(bf16[16,8,2048]{2,1,0:T(8,128)(2,1)} %copy.242), calls=%async_computation.8 | async-start | bytes 1048576 | tf_op jit(solution)/shard_map/all_to_all | solution.py:121
Sparse Core Ops, SparseCore 0:
  499.8 109.5 all-reduce.2
where the time goes:
time: 960 us; the launch traced here: 951 us
  waiting for transfers between devices  328 us (34%)
  matrix products  161 us (17%)
  local copies, waits for them, and re-layouts  159 us (17%)
  blocking collectives  157 us (16%)
  starting transfers between devices  112 us (12%)
  other arithmetic  19.3 us (2%)
  between operations  15 us (2%)
    psum x1, waiting for transfers between devices, body(): second_real, second_imag = lax.psum((second_real, second_imag), 'tp')  90.7 us
    all_to_all x1, blocking collectives, body(): lax.all_to_all(inverted[1][0], 'cp', split_axis=0, concat_axis=1, tiled=T...  52.8 us
    all_to_all x1, blocking collectives, body(): lax.all_to_all(inverted[0][0], 'cp', split_axis=0, concat_axis=1, tiled=T...  52.3 us
    all_to_all x1, blocking collectives, body(): lax.all_to_all(inverted[1][1], 'cp', split_axis=0, concat_axis=1, tiled=T...  52.2 us
    dot_general x10, matrix products, apply_table(): jnp.einsum(form, table_real, data_imag, precision=highest)  41.3 us
    all_to_all x1, waiting for transfers between devices, body(): lax.all_to_all(halves[2][0], 'cp', split_axis=1, concat_axis=0, tiled=True)  37 us
    all_to_all x1, waiting for transfers between devices, body(): lax.all_to_all(halves[2][1], 'cp', split_axis=1, concat_axis=0, tiled=True)  37 us
    all_to_all x1, waiting for transfers between devices, body(): lax.all_to_all(halves[0][0], 'cp', split_axis=1, concat_axis=0, tiled=True)  37 us
  transfers between devices with their start and end apart: 13, of which 11 were waited for; matrix products, arithmetic and copies ran while one was open for 17% of the time, Pallas kernels for 0%

commit v1 on v0

v1 whole, which is shorter than its diff:
```python
import functools
import math

import jax
import jax.numpy as jnp
import ml_dtypes
import numpy as np
from jax import lax
from jax.experimental import pallas as pl
from jax.experimental.pallas import tpu as pltpu
from jax.sharding import PartitionSpec as P

LANES = 128
FINE = 128
HALF = LANES // 2
both = ("tp", "cp")


def split(values):
    high = values.astype(ml_dtypes.bfloat16)
    low = (values - high.astype(np.float64)).astype(ml_dtypes.bfloat16)
    return high, low


def tables(coarse):
    total = coarse * FINE
    bins = np.arange(FINE, dtype=np.int64)[None, :, None]
    spots = coarse * np.arange(FINE, dtype=np.int64)[None, None, :] + np.arange(coarse, dtype=np.int64)[:, None, None]
    angle = ((4 * bins + 1) * spots % (4 * total)).astype(np.float64) * (2.0 * math.pi / (4 * total))
    table = np.concatenate([np.cos(angle), -np.sin(angle)], axis=1)
    high, low = split(table)
    forward = np.concatenate([high, low], axis=2)
    high, low = split(table.transpose(0, 2, 1) / total)
    inverse = np.concatenate([high, low, high], axis=2)
    return forward, inverse


def turned(real, imag, turn, size, sign):
    if turn == 0:
        return real, imag
    if 4 * turn == size:
        return (-sign * imag, sign * real) if sign < 0 else (-imag, real)
    if 8 * turn == size or 8 * turn == 3 * size:
        root = math.sqrt(0.5)
        same, cross = (real - sign * imag) * root, (imag + sign * real) * root
        return (same, cross) if 8 * turn == size else (-sign * cross, sign * same)
    cos, sin = math.cos(2 * math.pi * turn / size), sign * math.sin(2 * math.pi * turn / size)
    return real * cos - imag * sin, imag * cos + real * sin


def fourier(data, sign):
    size = len(data)
    if size == 1:
        return data
    even, odd = fourier(data[0::2], sign), fourier(data[1::2], sign)
    low, high = [], []
    for turn in range(size // 2):
        (er, ei), (tr, ti) = even[turn], turned(*odd[turn], turn, size, sign)
        low.append((er + tr, ei + ti))
        high.append((er - tr, ei - ti))
    return low + high


def left_lanes(shape):
    return lax.broadcasted_iota(jnp.int32, shape, 1) < HALF


def merge(left, right):
    return jnp.where(left_lanes(left.shape), left, pltpu.roll(right, HALF, 1))


def merge_right(left, right):
    return jnp.where(left_lanes(left.shape), pltpu.roll(left, HALF, 1), right)


def pack_kernel(part_ref, sig_ref, cot_ref, fil_ref, out_ref):
    rows = sig_ref.shape[0]
    quarter = rows // 4
    part = part_ref[0]
    sig, cot = sig_ref[...].astype(jnp.float32), cot_ref[...].astype(jnp.float32)
    out_ref[0, 0, :rows, :] = merge(sig, cot).astype(jnp.bfloat16)
    out_ref[1, 0, :rows, :] = merge_right(sig, cot).astype(jnp.bfloat16)
    start = pl.multiple_of(part * 2 * quarter, 2 * quarter)
    top = fil_ref[pl.ds(start, quarter), :].astype(jnp.float32)
    bottom = fil_ref[pl.ds(start + quarter, quarter), :].astype(jnp.float32)
    out_ref[0, 0, rows:, :] = merge(top, bottom).astype(jnp.bfloat16)
    out_ref[1, 0, rows:, :] = merge_right(top, bottom).astype(jnp.bfloat16)


def unpack_kernel(in_ref, sig_ref, fil_ref):
    first, second = in_ref[0, 0].astype(jnp.float32), in_ref[1, 0].astype(jnp.float32)
    sig_ref[...] = merge(first, second).astype(jnp.bfloat16)
    fil_ref[...] = merge_right(first, second).astype(jnp.bfloat16)


def gradients(forward_ref, inverse_ref, time_ref, freq_ref, cot_ref):
    coarse = forward_ref.shape[0]

    def onward(index, carry):
        rows = pl.ds(index, FINE, stride=coarse)
        for first, count in ((0, 2), (2, 1)):
            data = jnp.concatenate([time_ref[first + k, rows, :] for k in range(count)], axis=1).astype(jnp.bfloat16)
            bins = jnp.dot(forward_ref[index], jnp.concatenate([data, data], axis=0), preferred_element_type=jnp.float32)
            for k in range(count):
                freq_ref[first + k, index] = bins[:, k * LANES : (k + 1) * LANES]
        return carry

    lax.fori_loop(0, coarse, onward, 0)

    def middle(index, carry):
        real = pl.ds(pl.multiple_of(index * 8, 8), 8)
        imag = pl.ds(pl.multiple_of(index * 8 + FINE, 8), 8)

        def load(which):
            return [(freq_ref[which, c, real, :], freq_ref[which, c, imag, :]) for c in range(coarse)]

        for c, (cr, ci) in enumerate(fourier(load(1), -1)):
            cot_ref[c, real, :] = cr
            cot_ref[c, imag, :] = ci
        for source, target in ((2, 2), (0, 0)):
            products = []
            for c, (br, bi) in enumerate(fourier(load(source), -1)):
                cr, ci = cot_ref[c, real, :], cot_ref[c, imag, :]
                products.append((br * cr + bi * ci, br * ci - bi * cr))
            for c, (pr, pi) in enumerate(fourier(products, 1)):
                freq_ref[target, c, real, :] = pr
                freq_ref[target, c, imag, :] = pi
        return carry

    lax.fori_loop(0, FINE // 8, middle, 0)

    def back(index, carry):
        data = jnp.concatenate([freq_ref[2, index], freq_ref[0, index]], axis=1)
        high = data.astype(jnp.bfloat16)
        low = (data - high.astype(jnp.float32)).astype(jnp.bfloat16)
        values = jnp.dot(
            inverse_ref[index], jnp.concatenate([high, high, low], axis=0), preferred_element_type=jnp.float32
        )
        rows = pl.ds(index, FINE, stride=coarse)
        time_ref[0, rows, :] = values[:, :LANES]
        time_ref[1, rows, :] = values[:, LANES:]
        return carry

    lax.fori_loop(0, coarse, back, 0)


def packed_core(forward_ref, inverse_ref, in_ref, out_ref, time_ref, freq_ref, cot_ref):
    _, places, depth, _ = in_ref.shape
    rows = out_ref.shape[2]
    quarter = rows // 4

    def unfold(place, carry):
        start = pl.multiple_of(place * rows, rows)
        first, second = (in_ref[k, place, :rows, :].astype(jnp.float32) for k in range(2))
        time_ref[0, pl.ds(start, rows), :] = merge(first, second)
        time_ref[1, pl.ds(start, rows), :] = merge_right(first, second)
        for k in range(2):
            fold = in_ref[k, place, rows:, :].astype(jnp.float32)
            time_ref[2, pl.ds(start + 2 * k * quarter, quarter), :] = merge(fold, fold)
            time_ref[2, pl.ds(start + (2 * k + 1) * quarter, quarter), :] = merge_right(fold, fold)
        return carry

    lax.fori_loop(0, places, unfold, 0)
    gradients(forward_ref, inverse_ref, time_ref, freq_ref, cot_ref)

    def fold(place, carry):
        span = pl.ds(pl.multiple_of(place * rows, rows), rows)
        sig, fil = time_ref[0, span, :], time_ref[1, span, :]
        fil = fil + pltpu.roll(fil, HALF, 1)
        left = left_lanes(sig.shape)
        out_ref[0, place] = jnp.where(left, sig, fil).astype(jnp.bfloat16)
        out_ref[1, place] = jnp.where(left, pltpu.roll(sig, HALF, 1), fil).astype(jnp.bfloat16)
        return carry

    lax.fori_loop(0, places, fold, 0)


def plain_core(groups, forward_ref, inverse_ref, in_ref, out_ref, time_ref, freq_ref, cot_ref):
    time_ref[...] = in_ref[...].astype(jnp.float32)
    gradients(forward_ref, inverse_ref, time_ref, freq_ref, cot_ref)
    fil, step = time_ref[1], LANES // groups
    while step < LANES:
        fil, step = fil + pltpu.roll(fil, step, 1), 2 * step
    out_ref[0] = time_ref[0].astype(jnp.bfloat16)
    out_ref[1] = fil.astype(jnp.bfloat16)


def core(kernel, message, out_shape, total):
    coarse = total // FINE
    forward, inverse = tables(coarse)
    return pl.pallas_call(
        kernel,
        out_shape=jax.ShapeDtypeStruct(out_shape, jnp.bfloat16),
        scratch_shapes=[
            pltpu.VMEM((3, total, LANES), jnp.float32),
            pltpu.VMEM((3, coarse, 2 * FINE, LANES), jnp.float32),
            pltpu.VMEM((coarse, 2 * FINE, LANES), jnp.float32),
        ],
        compiler_params=pltpu.CompilerParams(vmem_limit_bytes=60 * 2**20),
        name="gradients",
    )(jnp.asarray(forward), jnp.asarray(inverse), message)


def exchange(message):
    return lax.all_to_all(message, both, split_axis=0, concat_axis=0, tiled=True)


def packed_body(signal, cotangent, long_filter):
    rows, columns = signal.shape
    places = lax.axis_size("cp")
    depth = rows + rows // 4
    column = pl.BlockSpec((rows, LANES), lambda j: (0, j))
    message = pl.pallas_call(
        pack_kernel,
        grid=(places,),
        in_specs=[pl.BlockSpec(memory_space=pltpu.SMEM), column, column, column],
        out_specs=pl.BlockSpec((2, 1, depth, LANES), lambda j: (0, j, 0, 0)),
        out_shape=jax.ShapeDtypeStruct((2, places, depth, LANES), jnp.bfloat16),
        name="pack",
    )(lax.axis_index("tp").reshape(1), signal, cotangent, long_filter)
    message = exchange(message.reshape(2 * places, depth, LANES)).reshape(2, places, depth, LANES)
    message = core(packed_core, message, (2, places, rows, LANES), rows * places)
    message = exchange(message.reshape(2 * places, rows, LANES)).reshape(2, places, rows, LANES)
    return pl.pallas_call(
        unpack_kernel,
        grid=(places,),
        in_specs=[pl.BlockSpec((2, 1, rows, LANES), lambda j: (0, j, 0, 0))],
        out_specs=[column, column],
        out_shape=[jax.ShapeDtypeStruct((rows, columns), jnp.bfloat16)] * 2,
        name="unpack",
    )(message)


def plain_body(signal, cotangent, long_filter):
    rows, columns = signal.shape
    groups, places = lax.axis_size("tp"), lax.axis_size("cp")
    total, width = rows * places, columns // (groups * places)

    def deal(block):
        return block.reshape(block.shape[0], groups * places, width).transpose(1, 0, 2).reshape(groups * places, -1)

    part = lax.axis_index("tp") * (rows // groups)
    share = lax.dynamic_slice_in_dim(long_filter, part, rows // groups, 0)
    message = exchange(jnp.concatenate([deal(signal), deal(cotangent), deal(share)], axis=1))
    sig, cot, fil = jnp.split(message, [rows * width, 2 * rows * width], axis=1)

    def arrange(block):
        block = block.reshape(groups, total, width).transpose(1, 0, 2)
        return jnp.pad(block, ((0, 0), (0, 0), (0, LANES // groups - width))).reshape(total, LANES)

    fil = fil.reshape(groups, places, rows // groups, width).transpose(1, 0, 2, 3).reshape(1, total, width)
    fil = jnp.broadcast_to(fil, (groups, total, width))
    data = jnp.stack([arrange(sig), arrange(cot), arrange(fil)])
    grads = core(functools.partial(plain_core, groups), data, (2, total, LANES), total)
    grads = grads.reshape(2, places, rows, groups, LANES // groups)[..., :width]
    message = exchange(grads.transpose(3, 1, 0, 2, 4).reshape(groups * places, 2 * rows * width))
    grads = message.reshape(groups * places, 2, rows, width).transpose(1, 2, 0, 3).reshape(2, rows, columns)
    return grads[0], grads[1]


def solution(mesh):
    groups, places = mesh.shape["tp"], mesh.shape["cp"]

    def body(signal, cotangent, long_filter):
        rows, columns = signal.shape
        packed = groups == 2 and columns == LANES * places and rows % 64 == 0
        return (packed_body if packed else plain_body)(signal, cotangent, long_filter)

    in_specs = (P("cp", "tp"), P("cp", "tp"), P("cp", None))
    out_specs = (P("cp", "tp"), P("cp", None))
    return jax.shard_map(body, mesh=mesh, in_specs=in_specs, out_specs=out_specs, check_vma=False)
```

time: 960 us -> 111 us (0.12)
  waiting for transfers between devices: 328 us -> 0 us
  matrix products: 161 us -> 0 us
  local copies, waits for them, and re-layouts: 159 us -> 0 us
  starting transfers between devices: 112 us -> 0 us
  blocking collectives: 157 us -> 70.7 us
  Pallas kernels: 0 us -> 37.6 us
  other arithmetic: 19.3 us -> 0 us
  between operations: 15 us -> 0.64 us
    all_to_all x12 -> x0, waiting for transfers between devices: 237 us -> none  [the longest x1 37 us: body(): lax.all_to_all(halves[2][0], 'cp', split_axis=1, concat_axis=0, tiled=True)]
    dot_general x50 -> x0, matrix products: 161 us -> none  [the longest x10 41.3 us: apply_table(): jnp.einsum(form, table_real, data_imag, precision=highest)]
    all_to_all x12 -> x0, starting transfers between devices: 112 us -> none  [the longest x1 16 us: body(): lax.all_to_all(shaped[2], 'cp', split_axis=1, concat_axis=0, tiled=True)]
    psum x1 -> x0, waiting for transfers between devices: 90.7 us -> none  [body(): second_real, second_imag = lax.psum((second_real, second_imag), 'tp')]
    all_to_all x3 -> x2, blocking collectives: 157 us -> 70.7 us  [exchange(): lax.all_to_all(message, both, split_axis=0, concat_axis=0, tiled=True)]
    all_to_all x18 -> x0, local copies, waits for them, and re-layouts: 57.4 us -> none  [the longest x3 9.52 us: body(): lax.all_to_all(inverted[1][0], 'cp', split_axis=0, concat_axis=1, tiled=T...]
    reshape x15 -> x0, local copies, waits for them, and re-layouts: 46.8 us -> none  [the longest x4 15.2 us: transform_rows(): part_real = data_real.reshape(outer, inner, -1)]
    pallas_call x0 -> x3, Pallas kernels: none -> 37.6 us  [the longest x1 19.2 us: core(): pl.pallas_call(kernel, out_shape=jax.ShapeDtypeStruct(out_shape, jnp.bflo...]
  transfers between devices with their start and end apart: 13 -> 0, of which waited for: 11 -> 0; matrix products, arithmetic and copies ran while one was open for 17% -> 0% of each run, Pallas kernels for 0% -> 0%
where the time goes in v1:
time: 111 us; the launch traced here: 109 us
  blocking collectives  70.7 us (64%)
  Pallas kernels  37.6 us (34%)
    all_to_all x2, blocking collectives, exchange(): lax.all_to_all(message, both, split_axis=0, concat_axis=0, tiled=True)  70.7 us
    pallas_call x1, Pallas kernels, core(): pl.pallas_call(kernel, out_shape=jax.ShapeDtypeStruct(out_shape, jnp.bflo...  19.2 us
    pallas_call x1, Pallas kernels, packed_body(): pl.pallas_call(unpack_kernel, grid=(places,), in_specs=[pl.BlockSpec((2,...  9.29 us
    pallas_call x1, Pallas kernels, packed_body(): pl.pallas_call(pack_kernel, grid=(places,), in_specs=[pl.BlockSpec(memory...  9.13 us

profile of v1, /device:TPU:0, one launch (start us, length us, event | category | flops | bytes accessed | tf_op | source)
XLA Modules:
  0.0 109.0 jit_solution(14468715444593678567)
XLA Ops:
  0.6 9.1 %pack.1 = bf16[2,16,160,128]{3,2,1,0:T(8,128)(2,1)} custom-call(s32[1]{0:T(128)} %bitcast.part_ref, bf16[128,2048]{1,0:T(8,128)(2,1)} %sig_ref.1, bf16[128,2048]{1,0:T(8,128)(2,1)} %cot_ref.1, bf16[128,2048]{1,0:T(8,128)(2,1)} %fil_ref.1), custom_call_target="tpu_custom_call" | custom-call | tf_op jit(solution)/shard_map/pack/pallas_call | solution.py:213
  9.8 40.2 %all_to_all.10 = bf16[32,160,128]{2,1,0:T(8,128)(2,1)} all-to-all(bf16[32,160,128]{2,1,0:T(8,128)(2,1)} %bitcast.5), channel_id=1, replica_groups=mesh['tp'=2,'cp'=16] {'tp','cp'}, dimensions={0} | all-to-all | bytes 2621440 | tf_op jit(solution)/shard_map/all_to_all | solution.py:205
  50.0 19.2 %gradients.1 = bf16[2,16,128,128]{3,2,1,0:T(8,128)(2,1)} custom-call(bf16[16,256,256]{2,1,0:T(8,128)(2,1)} %constant.10.clone.forward_ref, bf16[16,128,768]{2,1,0:T(8,128)(2,1)} %constant.11.clone.inverse_ref, bf16[2,16,160,128]{3,2,1,0:T(8,128)(2,1)} %bitcast.6), custom_call_target="tpu_custom_call" | custom-call | tf_op jit(solution)/shard_map/gradients/pallas_call | solution.py:191
  69.2 30.5 %all_to_all.11 = bf16[32,128,128]{2,1,0:T(8,128)(2,1)} all-to-all(bf16[32,128,128]{2,1,0:T(8,128)(2,1)} %bitcast.8), channel_id=1, replica_groups=mesh['tp'=2,'cp'=16] {'tp','cp'}, dimensions={0} | all-to-all | bytes 2097152 | tf_op jit(solution)/shard_map/all_to_all | solution.py:205
  99.7 9.3 %unpack.1 = (bf16[128,2048]{1,0:T(8,128)(2,1)}, bf16[128,2048]{1,0:T(8,128)(2,1)}) custom-call(bf16[2,16,128,128]{3,2,1,0:T(8,128)(2,1)} %bitcast.7), custom_call_target="tpu_custom_call" | custom-call | tf_op jit(solution)/shard_map/unpack/pallas_call | solution.py:224

commit v2 on v1

--- a/solution.py
+++ b/solution.py
@@ -76,21 +76,23 @@
 def pack_kernel(part_ref, sig_ref, cot_ref, fil_ref, out_ref):
     rows = sig_ref.shape[0]
     quarter = rows // 4
-    part = part_ref[0]
-    sig, cot = sig_ref[...].astype(jnp.float32), cot_ref[...].astype(jnp.float32)
-    out_ref[0, 0, :rows, :] = merge(sig, cot).astype(jnp.bfloat16)
-    out_ref[1, 0, :rows, :] = merge_right(sig, cot).astype(jnp.bfloat16)
-    start = pl.multiple_of(part * 2 * quarter, 2 * quarter)
-    top = fil_ref[pl.ds(start, quarter), :].astype(jnp.float32)
-    bottom = fil_ref[pl.ds(start + quarter, quarter), :].astype(jnp.float32)
-    out_ref[0, 0, rows:, :] = merge(top, bottom).astype(jnp.bfloat16)
-    out_ref[1, 0, rows:, :] = merge_right(top, bottom).astype(jnp.bfloat16)
+    start = pl.multiple_of(part_ref[0] * 2 * quarter, 2 * quarter)
+    for place in range(out_ref.shape[1]):
+        lanes = pl.ds(place * LANES, LANES)
+        sig, cot = sig_ref[:, lanes], cot_ref[:, lanes]
+        out_ref[0, place, :rows, :] = merge(sig, cot)
+        out_ref[1, place, :rows, :] = merge_right(sig, cot)
+        top, bottom = fil_ref[pl.ds(start, quarter), lanes], fil_ref[pl.ds(start + quarter, quarter), lanes]
+        out_ref[0, place, rows:, :] = merge(top, bottom)
+        out_ref[1, place, rows:, :] = merge_right(top, bottom)
 
 
 def unpack_kernel(in_ref, sig_ref, fil_ref):
-    first, second = in_ref[0, 0].astype(jnp.float32), in_ref[1, 0].astype(jnp.float32)
-    sig_ref[...] = merge(first, second).astype(jnp.bfloat16)
-    fil_ref[...] = merge_right(first, second).astype(jnp.bfloat16)
+    for place in range(in_ref.shape[1]):
+        lanes = pl.ds(place * LANES, LANES)
+        first, second = in_ref[0, place], in_ref[1, place]
+        sig_ref[:, lanes] = merge(first, second)
+        fil_ref[:, lanes] = merge_right(first, second)
 
 
 def gradients(forward_ref, inverse_ref, time_ref, freq_ref, cot_ref):
@@ -105,7 +107,7 @@
                 freq_ref[first + k, index] = bins[:, k * LANES : (k + 1) * LANES]
         return carry
 
-    lax.fori_loop(0, coarse, onward, 0)
+    lax.fori_loop(0, coarse, onward, 0, unroll=16)
 
     def middle(index, carry):
         real = pl.ds(pl.multiple_of(index * 8, 8), 8)
@@ -127,7 +129,7 @@
                 freq_ref[target, c, imag, :] = pi
         return carry
 
-    lax.fori_loop(0, FINE // 8, middle, 0)
+    lax.fori_loop(0, FINE // 8, middle, 0, unroll=4)
 
     def back(index, carry):
         data = jnp.concatenate([freq_ref[2, index], freq_ref[0, index]], axis=1)
@@ -141,7 +143,7 @@
         time_ref[1, rows, :] = values[:, LANES:]
         return carry
 
-    lax.fori_loop(0, coarse, back, 0)
+    lax.fori_loop(0, coarse, back, 0, unroll=16)
 
 
 def packed_core(forward_ref, inverse_ref, in_ref, out_ref, time_ref, freq_ref, cot_ref):
@@ -160,7 +162,7 @@
             time_ref[2, pl.ds(start + (2 * k + 1) * quarter, quarter), :] = merge_right(fold, fold)
         return carry
 
-    lax.fori_loop(0, places, unfold, 0)
+    lax.fori_loop(0, places, unfold, 0, unroll=16)
     gradients(forward_ref, inverse_ref, time_ref, freq_ref, cot_ref)
 
     def fold(place, carry):
@@ -172,7 +174,7 @@
         out_ref[1, place] = jnp.where(left, pltpu.roll(sig, HALF, 1), fil).astype(jnp.bfloat16)
         return carry
 
-    lax.fori_loop(0, places, fold, 0)
+    lax.fori_loop(0, places, fold, 0, unroll=16)
 
 
 def plain_core(groups, forward_ref, inverse_ref, in_ref, out_ref, time_ref, freq_ref, cot_ref):
@@ -196,7 +198,7 @@
             pltpu.VMEM((3, coarse, 2 * FINE, LANES), jnp.float32),
             pltpu.VMEM((coarse, 2 * FINE, LANES), jnp.float32),
         ],
-        compiler_params=pltpu.CompilerParams(vmem_limit_bytes=60 * 2**20),
+        compiler_params=pltpu.CompilerParams(vmem_limit_bytes=total * 11 * 2**10),
         name="gradients",
     )(jnp.asarray(forward), jnp.asarray(inverse), message)
 
@@ -209,12 +211,14 @@
     rows, columns = signal.shape
     places = lax.axis_size("cp")
     depth = rows + rows // 4
-    column = pl.BlockSpec((rows, LANES), lambda j: (0, j))
+    steps = 2
+    block = places // steps
+    column = pl.BlockSpec((rows, columns // steps), lambda j: (0, j))
     message = pl.pallas_call(
         pack_kernel,
-        grid=(places,),
+        grid=(steps,),
         in_specs=[pl.BlockSpec(memory_space=pltpu.SMEM), column, column, column],
-        out_specs=pl.BlockSpec((2, 1, depth, LANES), lambda j: (0, j, 0, 0)),
+        out_specs=pl.BlockSpec((2, block, depth, LANES), lambda j: (0, j, 0, 0)),
         out_shape=jax.ShapeDtypeStruct((2, places, depth, LANES), jnp.bfloat16),
         name="pack",
     )(lax.axis_index("tp").reshape(1), signal, cotangent, long_filter)
@@ -223,8 +227,8 @@
     message = exchange(message.reshape(2 * places, rows, LANES)).reshape(2, places, rows, LANES)
     return pl.pallas_call(
         unpack_kernel,
-        grid=(places,),
-        in_specs=[pl.BlockSpec((2, 1, rows, LANES), lambda j: (0, j, 0, 0))],
+        grid=(steps,),
+        in_specs=[pl.BlockSpec((2, block, rows, LANES), lambda j: (0, j, 0, 0))],
         out_specs=[column, column],
         out_shape=[jax.ShapeDtypeStruct((rows, columns), jnp.bfloat16)] * 2,
         name="unpack",

time: 111 us -> 82.8 us (0.75); the launches traced: 109 us -> 82.6 us
  Pallas kernels: 37.6 us -> 12.3 us
    pallas_call x2, Pallas kernels: 18.4 us -> 4.94 us  [the longest x1 2.65 us: packed_body(): pl.pallas_call(pack_kernel, grid=(steps,), in_specs=[pl.BlockSpec(memory_...]
    pallas_call x1, Pallas kernels: 19.2 us -> 7.33 us  [core(): pl.pallas_call(kernel, out_shape=jax.ShapeDtypeStruct(out_shape, jnp.bflo...]
where the time goes in v2:
time: 82.8 us; the launch traced here: 82.6 us
  blocking collectives  69.7 us (84%)
  Pallas kernels  12.3 us (15%)
    all_to_all x2, blocking collectives, exchange(): lax.all_to_all(message, both, split_axis=0, concat_axis=0, tiled=True)  69.7 us
    pallas_call x1, Pallas kernels, core(): pl.pallas_call(kernel, out_shape=jax.ShapeDtypeStruct(out_shape, jnp.bflo...  7.33 us
    pallas_call x1, Pallas kernels, packed_body(): pl.pallas_call(pack_kernel, grid=(steps,), in_specs=[pl.BlockSpec(memory_...  2.65 us
    pallas_call x1, Pallas kernels, packed_body(): pl.pallas_call(unpack_kernel, grid=(steps,), in_specs=[pl.BlockSpec((2, b...  2.29 us

profile of v2, /device:TPU:0, one launch (start us, length us, event | category | flops | bytes accessed | tf_op | source)
XLA Modules:
  0.0 82.6 jit_solution(15310586139539209651)
XLA Ops:
  0.6 0.0 copy-start
  0.6 2.6 %pack.1 = bf16[2,16,160,128]{3,2,1,0:T(8,128)(2,1)} custom-call(s32[1]{0:T(128)} %bitcast.part_ref, bf16[128,2048]{1,0:T(8,128)(2,1)} %sig_ref.1, bf16[128,2048]{1,0:T(8,128)(2,1)} %cot_ref.1, bf16[128,2048]{1,0:T(8,128)(2,1)} %fil_ref.1), custom_call_target="tpu_custom_call" | custom-call | tf_op jit(solution)/shard_map/pack/pallas_call | solution.py:217
  3.3 0.0 copy-start.1
  3.3 40.1 %all_to_all.10 = bf16[32,160,128]{2,1,0:T(8,128)(2,1)S(1)} all-to-all(bf16[32,160,128]{2,1,0:T(8,128)(2,1)} %bitcast.7), channel_id=1, replica_groups=mesh['tp'=2,'cp'=16] {'tp','cp'}, dimensions={0} | all-to-all | bytes 2621440 | tf_op jit(solution)/shard_map/all_to_all | solution.py:207
  43.4 0.0 copy-done
  43.4 0.0 copy-done.1
  43.4 7.3 %gradients.1 = bf16[2,16,128,128]{3,2,1,0:T(8,128)(2,1)S(1)} custom-call(bf16[16,256,256]{2,1,0:T(8,128)(2,1)S(1)} %copy-done.1, bf16[16,128,768]{2,1,0:T(8,128)(2,1)S(1)} %copy-done, bf16[2,16,160,128]{3,2,1,0:T(8,128)(2,1)S(1)} %bitcast.5), custom_call_target="tpu_custom_call" | custom-call | tf_op jit(solution)/shard_map/gradients/pallas_call | solution.py:193
  50.7 29.6 %all_to_all.11 = bf16[32,128,128]{2,1,0:T(8,128)(2,1)} all-to-all(bf16[32,128,128]{2,1,0:T(8,128)(2,1)S(1)} %bitcast.6), channel_id=1, replica_groups=mesh['tp'=2,'cp'=16] {'tp','cp'}, dimensions={0} | all-to-all | bytes 2097152 | tf_op jit(solution)/shard_map/all_to_all | solution.py:207
  80.3 2.3 %unpack.1 = (bf16[128,2048]{1,0:T(8,128)(2,1)}, bf16[128,2048]{1,0:T(8,128)(2,1)}) custom-call(bf16[2,16,128,128]{3,2,1,0:T(8,128)(2,1)} %bitcast.8), custom_call_target="tpu_custom_call" | custom-call | tf_op jit(solution)/shard_map/unpack/pallas_call | solution.py:228
Async XLA Ops:
  0.6 42.8 %copy-start = (bf16[16,128,768]{2,1,0:T(8,128)(2,1)S(1)}, bf16[16,128,768]{2,1,0:T(8,128)(2,1)}, u32[]{:S(2)}) copy-start(bf16[16,128,768]{2,1,0:T(8,128)(2,1)} %constant.11.clone.inverse_ref) | copy-start | bytes 9437188
  3.3 40.1 %copy-start.1 = (bf16[16,256,256]{2,1,0:T(8,128)(2,1)S(1)}, bf16[16,256,256]{2,1,0:T(8,128)(2,1)}, u32[]{:S(2)}) copy-start(bf16[16,256,256]{2,1,0:T(8,128)(2,1)} %constant.10.clone.forward_ref) | copy-start | bytes 6291460

commit v3 on v2

v3 whole, which is shorter than its diff:
```python
import functools
import math

import jax
import jax.numpy as jnp
import ml_dtypes
import numpy as np
from jax import lax
from jax.experimental import pallas as pl
from jax.experimental.pallas import tpu as pltpu
from jax.sharding import PartitionSpec as P

LANES = 128
FINE = 128
HALF = LANES // 2
SLAB = 8
both = ("tp", "cp")


def split(values):
    high = values.astype(ml_dtypes.bfloat16)
    low = (values - high.astype(np.float64)).astype(ml_dtypes.bfloat16)
    return high, low


def tables(coarse):
    total = coarse * FINE
    bins = np.arange(FINE, dtype=np.int64)[None, :, None]
    spots = coarse * np.arange(FINE, dtype=np.int64)[None, None, :] + np.arange(coarse, dtype=np.int64)[:, None, None]
    angle = ((4 * bins + 1) * spots % (4 * total)).astype(np.float64) * (2.0 * math.pi / (4 * total))
    table = np.concatenate([np.cos(angle), -np.sin(angle)], axis=1)
    forward = np.concatenate(split(table), axis=2)
    inverse = np.concatenate(split(table.transpose(0, 2, 1) / total), axis=2)
    return forward, inverse


def butterfly(even, odd, turn, size, sign):
    (er, ei), (dr, di) = even, odd
    if turn == 0:
        return (er + dr, ei + di), (er - dr, ei - di)
    if 4 * turn == size:
        back, forth = (er + di, ei - dr), (er - di, ei + dr)
        return (back, forth) if sign < 0 else (forth, back)
    if 8 * turn in (size, 3 * size):
        root = math.sqrt(0.5)
        total, gap = (dr + di) * root, ((di - dr) if sign < 0 else (dr - di)) * root
        if sign < 0 and 8 * turn == size:
            return (er + total, ei + gap), (er - total, ei - gap)
        if sign < 0:
            return (er + gap, ei - total), (er - gap, ei + total)
        if 8 * turn == size:
            return (er + gap, ei + total), (er - gap, ei - total)
        return (er - total, ei + gap), (er + total, ei - gap)
    cos, sin = math.cos(2 * math.pi * turn / size), sign * math.sin(2 * math.pi * turn / size)
    dr, di = dr * cos - di * sin, di * cos + dr * sin
    return (er + dr, ei + di), (er - dr, ei - di)


def fourier(data, sign):
    size = len(data)
    if size == 1:
        return data
    even, odd = fourier(data[0::2], sign), fourier(data[1::2], sign)
    pairs = [butterfly(even[turn], odd[turn], turn, size, sign) for turn in range(size // 2)]
    return [low for low, _ in pairs] + [high for _, high in pairs]


def left_lanes(shape):
    return lax.broadcasted_iota(jnp.int32, shape, 1) < HALF


def merge(left, right):
    return jnp.where(left_lanes(left.shape), left, pltpu.roll(right, HALF, 1))


def merge_right(left, right):
    return jnp.where(left_lanes(left.shape), pltpu.roll(left, HALF, 1), right)


def pack_kernel(part_ref, sig_ref, cot_ref, fil_ref, out_ref):
    rows = sig_ref.shape[0]
    quarter = rows // 4
    start = pl.multiple_of(part_ref[0] * 2 * quarter, 2 * quarter)
    for place in range(out_ref.shape[1]):
        lanes = pl.ds(place * LANES, LANES)
        sig, cot = sig_ref[:, lanes], cot_ref[:, lanes]
        out_ref[0, place, :rows, :] = merge(sig, cot)
        out_ref[1, place, :rows, :] = merge_right(sig, cot)
        top, bottom = fil_ref[pl.ds(start, quarter), lanes], fil_ref[pl.ds(start + quarter, quarter), lanes]
        out_ref[0, place, rows:, :] = merge(top, bottom)
        out_ref[1, place, rows:, :] = merge_right(top, bottom)


def unpack_kernel(in_ref, sig_ref, fil_ref):
    for place in range(in_ref.shape[1]):
        lanes = pl.ds(place * LANES, LANES)
        first, second = in_ref[0, place], in_ref[1, place]
        sig_ref[:, lanes] = merge(first, second)
        fil_ref[:, lanes] = merge_right(first, second)


def onward(table_ref, time_refs, freq_refs, index):
    rows = pl.ds(index, FINE, stride=table_ref.shape[0])
    data = jnp.concatenate([ref[rows, :] for ref in time_refs], axis=1).astype(jnp.bfloat16)
    data = jnp.concatenate([data, data], axis=0)
    data = jnp.dot(table_ref[index], data, preferred_element_type=jnp.float32)
    for k, ref in enumerate(freq_refs):
        ref[index] = data[:, k * LANES : (k + 1) * LANES]


def back(table_ref, freq_refs, time_refs, index):
    rows = pl.ds(index, FINE, stride=table_ref.shape[0])
    data = jnp.concatenate([ref[index] for ref in freq_refs], axis=1)
    high = data.astype(jnp.bfloat16)
    low = (data - high.astype(jnp.float32)).astype(jnp.bfloat16)
    table = table_ref[index]
    table = jnp.concatenate([table, table[:, : 2 * FINE]], axis=1)
    data = jnp.concatenate([high, high, low], axis=0)
    data = jnp.dot(table, data, preferred_element_type=jnp.float32)
    for k, ref in enumerate(time_refs):
        ref[rows, :] = data[:, k * LANES : (k + 1) * LANES]


def rows_of(index):
    start = pl.multiple_of(index * SLAB, SLAB)
    return pl.ds(start, SLAB), pl.ds(start + FINE, SLAB)


def load(freq_ref, index):
    real, imag = rows_of(index)
    return [(freq_ref[c, real, :], freq_ref[c, imag, :]) for c in range(freq_ref.shape[0])]


def store(freq_ref, index, data):
    real, imag = rows_of(index)
    for c, (dr, di) in enumerate(data):
        freq_ref[c, real, :] = dr
        freq_ref[c, imag, :] = di


def spectrum(freq_ref, index):
    store(freq_ref, index, fourier(load(freq_ref, index), -1))


def correlate(freq_ref, cot_ref, index):
    real, imag = rows_of(index)
    products = []
    for c, (br, bi) in enumerate(fourier(load(freq_ref, index), -1)):
        cr, ci = cot_ref[c, real, :], cot_ref[c, imag, :]
        products.append((br * cr + bi * ci, br * ci - bi * cr))
    store(freq_ref, index, fourier(products, 1))


def each(count, step, unroll):
    def body(index, carry):
        step(index)
        return carry

    lax.fori_loop(0, count, body, 0, unroll=min(unroll, count))


def gradients(forward_ref, inverse_ref, times, freqs, fetch):
    sig_time, cot_time, fil_time = times
    sig_freq, cot_freq, fil_freq = freqs
    coarse = forward_ref.shape[0]

    def beside(matrix, vector, unroll):
        def step(index):
            matrix(index)
            if coarse * SLAB == FINE:
                vector(index)
            else:
                pl.when(index < FINE // SLAB)(lambda: vector(index))

        each(coarse, step, unroll)

    each(coarse, lambda i: onward(forward_ref, (cot_time,), (cot_freq,), i), UNROLL[0])
    beside(
        lambda i: onward(forward_ref, (fil_time, sig_time), (fil_freq, sig_freq), i),
        lambda i: spectrum(cot_freq, i),
        UNROLL[1],
    )
    each(FINE // SLAB, lambda i: correlate(fil_freq, cot_freq, i), UNROLL[2])
    each(FINE // SLAB, lambda i: correlate(sig_freq, cot_freq, i), UNROLL[3])
    fetch.wait()
    each(coarse, lambda i: back(inverse_ref, (sig_freq, fil_freq), (sig_time, fil_time), i), UNROLL[4])


UNROLL = (16, 16, 4, 4, 16)


def packed_core(forward_ref, inverse_hbm, in_ref, out_ref, inverse_ref, arrived, *scratch):
    times, freqs = scratch[:3], scratch[3:]
    _, places, depth, _ = in_ref.shape
    rows = out_ref.shape[2]
    quarter = rows // 4
    fetch = pltpu.make_async_copy(inverse_hbm, inverse_ref, arrived)
    fetch.start()

    def unfold(place):
        start = pl.multiple_of(place * rows, rows)
        first, second = (in_ref[k, place, :rows, :].astype(jnp.float32) for k in range(2))
        times[0][pl.ds(start, rows), :] = merge(first, second)
        times[1][pl.ds(start, rows), :] = merge_right(first, second)
        for k in range(2):
            fold = in_ref[k, place, rows:, :].astype(jnp.float32)
            times[2][pl.ds(start + 2 * k * quarter, quarter), :] = merge(fold, fold)
            times[2][pl.ds(start + (2 * k + 1) * quarter, quarter), :] = merge_right(fold, fold)

    each(places, unfold, 16)
    gradients(forward_ref, inverse_ref, times, freqs, fetch)

    def fold(place):
        span = pl.ds(pl.multiple_of(place * rows, rows), rows)
        sig, fil = times[2][span, :], times[0][span, :]
        fil = fil + pltpu.roll(fil, HALF, 1)
        left = left_lanes(sig.shape)
        out_ref[0, place] = jnp.where(left, sig, fil).astype(jnp.bfloat16)
        out_ref[1, place] = jnp.where(left, pltpu.roll(sig, HALF, 1), fil).astype(jnp.bfloat16)

    each(places, fold, 16)


def plain_core(groups, forward_ref, inverse_hbm, in_ref, out_ref, inverse_ref, arrived, *scratch):
    times, freqs = scratch[:3], scratch[3:]
    fetch = pltpu.make_async_copy(inverse_hbm, inverse_ref, arrived)
    fetch.start()
    for k in range(3):
        times[k][...] = in_ref[k].astype(jnp.float32)
    gradients(forward_ref, inverse_ref, times, freqs, fetch)
    fil, step = times[0][...], LANES // groups
    while step < LANES:
        fil, step = fil + pltpu.roll(fil, step, 1), 2 * step
    out_ref[0] = times[2][...].astype(jnp.bfloat16)
    out_ref[1] = fil.astype(jnp.bfloat16)


def core(kernel, message, out_shape, total):
    coarse = total // FINE
    forward, inverse = tables(coarse)
    vmem = pl.BlockSpec(memory_space=pltpu.VMEM)
    return pl.pallas_call(
        kernel,
        in_specs=[vmem, pl.BlockSpec(memory_space=pltpu.HBM), vmem],
        out_specs=vmem,
        out_shape=pltpu.VMEM(out_shape, jnp.bfloat16),
        scratch_shapes=[pltpu.VMEM(inverse.shape, jnp.bfloat16), pltpu.SemaphoreType.DMA]
        + [pltpu.VMEM((total, LANES), jnp.float32)] * 3
        + [pltpu.VMEM((coarse, 2 * FINE, LANES), jnp.float32)] * 3,
        compiler_params=pltpu.CompilerParams(vmem_limit_bytes=total * 11 * 2**10),
        name="gradients",
    )(jnp.asarray(forward), jnp.asarray(inverse), pltpu.with_memory_space_constraint(message, pltpu.VMEM))


def exchange(message):
    return lax.all_to_all(message, both, split_axis=0, concat_axis=0, tiled=True)


def packed_body(signal, cotangent, long_filter):
    rows, columns = signal.shape
    places = lax.axis_size("cp")
    depth = rows + rows // 4
    steps = 2
    block = places // steps
    column = pl.BlockSpec((rows, columns // steps), lambda j: (0, j))
    message = pl.pallas_call(
        pack_kernel,
        grid=(steps,),
        in_specs=[pl.BlockSpec(memory_space=pltpu.SMEM), column, column, column],
        out_specs=pl.BlockSpec((2, block, depth, LANES), lambda j: (0, j, 0, 0)),
        out_shape=pltpu.VMEM((2, places, depth, LANES), jnp.bfloat16),
        name="pack",
    )(lax.axis_index("tp").reshape(1), signal, cotangent, long_filter)
    message = exchange(message.reshape(2 * places, depth, LANES)).reshape(2, places, depth, LANES)
    message = core(packed_core, message, (2, places, rows, LANES), rows * places)
    message = exchange(message.reshape(2 * places, rows, LANES)).reshape(2, places, rows, LANES)
    return pl.pallas_call(
        unpack_kernel,
        grid=(steps,),
        in_specs=[pl.BlockSpec((2, block, rows, LANES), lambda j: (0, j, 0, 0))],
        out_specs=[column, column],
        out_shape=[jax.ShapeDtypeStruct((rows, columns), jnp.bfloat16)] * 2,
        name="unpack",
    )(pltpu.with_memory_space_constraint(message, pltpu.VMEM))


def plain_body(signal, cotangent, long_filter):
    rows, columns = signal.shape
    groups, places = lax.axis_size("tp"), lax.axis_size("cp")
    total, width = rows * places, columns // (groups * places)

    def deal(block):
        return block.reshape(block.shape[0], groups * places, width).transpose(1, 0, 2).reshape(groups * places, -1)

    part = lax.axis_index("tp") * (rows // groups)
    share = lax.dynamic_slice_in_dim(long_filter, part, rows // groups, 0)
    message = exchange(jnp.concatenate([deal(signal), deal(cotangent), deal(share)], axis=1))
    sig, cot, fil = jnp.split(message, [rows * width, 2 * rows * width], axis=1)

    def arrange(block):
        block = block.reshape(groups, total, width).transpose(1, 0, 2)
        return jnp.pad(block, ((0, 0), (0, 0), (0, LANES // groups - width))).reshape(total, LANES)

    fil = fil.reshape(groups, places, rows // groups, width).transpose(1, 0, 2, 3).reshape(1, total, width)
    fil = jnp.broadcast_to(fil, (groups, total, width))
    data = jnp.stack([arrange(sig), arrange(cot), arrange(fil)])
    grads = core(functools.partial(plain_core, groups), data, (2, total, LANES), total)
    grads = grads.reshape(2, places, rows, groups, LANES // groups)[..., :width]
    message = exchange(grads.transpose(3, 1, 0, 2, 4).reshape(groups * places, 2 * rows * width))
    grads = message.reshape(groups * places, 2, rows, width).transpose(1, 2, 0, 3).reshape(2, rows, columns)
    return grads[0], grads[1]


def solution(mesh):
    groups, places = mesh.shape["tp"], mesh.shape["cp"]

    def body(signal, cotangent, long_filter):
        rows, columns = signal.shape
        packed = groups == 2 and columns == LANES * places and rows % 64 == 0
        return (packed_body if packed else plain_body)(signal, cotangent, long_filter)

    in_specs = (P("cp", "tp"), P("cp", "tp"), P("cp", None))
    out_specs = (P("cp", "tp"), P("cp", None))
    return jax.shard_map(body, mesh=mesh, in_specs=in_specs, out_specs=out_specs, check_vma=False)
```

time: 82.8 us -> 80.2 us (0.969)
  Pallas kernels: 12.3 us -> 10 us
    pallas_call x1, Pallas kernels: 2.29 us -> 1.33 us  [packed_body(): pl.pallas_call(unpack_kernel, grid=(steps,), in_specs=[pl.BlockSpec((2, b...]
where the time goes in v3:
time: 80.2 us; the launch traced here: 80.1 us
  blocking collectives  69.3 us (86%)
  Pallas kernels  10 us (12%)
    all_to_all x2, blocking collectives, exchange(): lax.all_to_all(message, both, split_axis=0, concat_axis=0, tiled=True)  69.3 us
    pallas_call x1, Pallas kernels, core(): pl.pallas_call(kernel, in_specs=[vmem, pl.BlockSpec(memory_space=pltpu.HB...  6.84 us
    pallas_call x1, Pallas kernels, packed_body(): pl.pallas_call(pack_kernel, grid=(steps,), in_specs=[pl.BlockSpec(memory_...  1.86 us

profile of v3, /device:TPU:0, one launch (start us, length us, event | category | flops | bytes accessed | tf_op | source)
XLA Modules:
  0.0 80.1 jit_solution(11918833648183534155)
XLA Ops:
  0.6 0.0 copy-start
  0.6 1.9 %pack.1 = bf16[2,16,160,128]{3,2,1,0:T(8,128)(2,1)S(1)} custom-call(s32[1]{0:T(128)} %bitcast.part_ref, bf16[128,2048]{1,0:T(8,128)(2,1)} %sig_ref.1, bf16[128,2048]{1,0:T(8,128)(2,1)} %cot_ref.1, bf16[128,2048]{1,0:T(8,128)(2,1)} %fil_ref.1), custom_call_target="tpu_custom_call" | custom-call | tf_op jit(solution)/shard_map/pack/pallas_call | solution.py:266
  2.5 0.0 copy-start.1
  2.5 39.9 %all_to_all.10 = bf16[32,160,128]{2,1,0:T(8,128)(2,1)S(1)} all-to-all(bf16[32,160,128]{2,1,0:T(8,128)(2,1)S(1)} %bitcast.5), channel_id=1, replica_groups=mesh['tp'=2,'cp'=16] {'tp','cp'}, dimensions={0} | all-to-all | bytes 2621440 | tf_op jit(solution)/shard_map/all_to_all | solution.py:256
  42.4 0.0 copy-done
  42.4 0.0 copy-done.1
  42.4 6.8 %gradients.1 = bf16[2,16,128,128]{3,2,1,0:T(8,128)(2,1)S(1)} custom-call(bf16[16,256,256]{2,1,0:T(8,128)(2,1)S(1)} %copy-done.1, bf16[16,128,512]{2,1,0:T(8,128)(2,1)S(1)} %copy-done, bf16[2,16,160,128]{3,2,1,0:T(8,128)(2,1)S(1)} %bitcast.6), custom_call_target="tpu_custom_call" | custom-call | tf_op jit(solution)/shard_map/gradients/pallas_call | solution.py:242
  49.3 29.4 %all_to_all.11 = bf16[32,128,128]{2,1,0:T(8,128)(2,1)S(1)} all-to-all(bf16[32,128,128]{2,1,0:T(8,128)(2,1)S(1)} %bitcast.7), channel_id=1, replica_groups=mesh['tp'=2,'cp'=16] {'tp','cp'}, dimensions={0} | all-to-all | bytes 2097152 | tf_op jit(solution)/shard_map/all_to_all | solution.py:256
  78.7 1.3 %unpack.1 = (bf16[128,2048]{1,0:T(8,128)(2,1)}, bf16[128,2048]{1,0:T(8,128)(2,1)}) custom-call(bf16[2,16,128,128]{3,2,1,0:T(8,128)(2,1)S(1)} %bitcast.8), custom_call_target="tpu_custom_call" | custom-call | tf_op jit(solution)/shard_map/unpack/pallas_call | solution.py:277
Async XLA Ops:
  0.6 41.8 %copy-start = (bf16[16,128,512]{2,1,0:T(8,128)(2,1)S(1)}, bf16[16,128,512]{2,1,0:T(8,128)(2,1)}, u32[]{:S(2)}) copy-start(bf16[16,128,512]{2,1,0:T(8,128)(2,1)} %constant.11.clone.inverse_hbm) | copy-start | bytes 6291460
  2.5 39.9 %copy-start.1 = (bf16[16,256,256]{2,1,0:T(8,128)(2,1)S(1)}, bf16[16,256,256]{2,1,0:T(8,128)(2,1)}, u32[]{:S(2)}) copy-start(bf16[16,256,256]{2,1,0:T(8,128)(2,1)} %constant.10.clone.forward_ref) | copy-start | bytes 6291460

commit v4 on v3

--- a/solution.py
+++ b/solution.py
@@ -14,6 +14,8 @@
 FINE = 128
 HALF = LANES // 2
 SLAB = 8
+IN_CHUNKS = 2
+OUT_CHUNKS = 4
 both = ("tp", "cp")
 
 
@@ -77,39 +79,71 @@
     return jnp.where(left_lanes(left.shape), pltpu.roll(left, HALF, 1), right)
 
 
-def pack_kernel(part_ref, sig_ref, cot_ref, fil_ref, out_ref):
-    rows = sig_ref.shape[0]
+def pack_kernel(part_ref, sig_hbm, cot_hbm, fil_hbm, out_ref, sig_ref, cot_ref, fil_ref, arrived):
+    rows, columns = sig_ref.shape
     quarter = rows // 4
     start = pl.multiple_of(part_ref[0] * 2 * quarter, 2 * quarter)
-    for place in range(out_ref.shape[1]):
-        lanes = pl.ds(place * LANES, LANES)
-        sig, cot = sig_ref[:, lanes], cot_ref[:, lanes]
-        out_ref[0, place, :rows, :] = merge(sig, cot)
-        out_ref[1, place, :rows, :] = merge_right(sig, cot)
-        top, bottom = fil_ref[pl.ds(start, quarter), lanes], fil_ref[pl.ds(start + quarter, quarter), lanes]
-        out_ref[0, place, rows:, :] = merge(top, bottom)
-        out_ref[1, place, rows:, :] = merge_right(top, bottom)
-
-
-def unpack_kernel(in_ref, sig_ref, fil_ref):
-    for place in range(in_ref.shape[1]):
-        lanes = pl.ds(place * LANES, LANES)
-        first, second = in_ref[0, place], in_ref[1, place]
-        sig_ref[:, lanes] = merge(first, second)
-        fil_ref[:, lanes] = merge_right(first, second)
+    chunk = columns // IN_CHUNKS
+    copies = []
+    for c in range(IN_CHUNKS):
+        lanes = pl.ds(c * chunk, chunk)
+        copies.append(
+            (
+                pltpu.make_async_copy(sig_hbm.at[:, lanes], sig_ref.at[:, lanes], arrived.at[0, c]),
+                pltpu.make_async_copy(cot_hbm.at[:, lanes], cot_ref.at[:, lanes], arrived.at[1, c]),
+                pltpu.make_async_copy(
+                    fil_hbm.at[pl.ds(start, 2 * quarter), lanes], fil_ref.at[:, lanes], arrived.at[2, c]
+                ),
+            )
+        )
+        for copy in copies[c]:
+            copy.start()
+    for c in range(IN_CHUNKS):
+        for copy in copies[c]:
+            copy.wait()
+        for place in range(c * chunk // LANES, (c + 1) * chunk // LANES):
+            lanes = pl.ds(place * LANES, LANES)
+            sig, cot = sig_ref[:, lanes], cot_ref[:, lanes]
+            out_ref[0, place, :rows, :] = merge(sig, cot)
+            out_ref[1, place, :rows, :] = merge_right(sig, cot)
+            top, bottom = fil_ref[:quarter, lanes], fil_ref[quarter:, lanes]
+            out_ref[0, place, rows:, :] = merge(top, bottom)
+            out_ref[1, place, rows:, :] = merge_right(top, bottom)
+
+
+def unpack_kernel(in_ref, sig_hbm, fil_hbm, sig_ref, fil_ref, sent):
+    columns = sig_ref.shape[1]
+    chunk = columns // OUT_CHUNKS
+    copies = []
+    for c in range(OUT_CHUNKS):
+        for place in range(c * chunk // LANES, (c + 1) * chunk // LANES):
+            lanes = pl.ds(place * LANES, LANES)
+            first, second = in_ref[0, place], in_ref[1, place]
+            sig_ref[:, lanes] = merge(first, second)
+            fil_ref[:, lanes] = merge_right(first, second)
+        lanes = pl.ds(c * chunk, chunk)
+        copies.append(pltpu.make_async_copy(sig_ref.at[:, lanes], sig_hbm.at[:, lanes], sent.at[0, c]))
+        copies.append(pltpu.make_async_copy(fil_ref.at[:, lanes], fil_hbm.at[:, lanes], sent.at[1, c]))
+        copies[-2].start()
+        copies[-1].start()
+    for copy in copies:
+        copy.wait()
+
+
+def pitch(coarse):
+    return coarse + 8
 
 
 def onward(table_ref, time_refs, freq_refs, index):
-    rows = pl.ds(index, FINE, stride=table_ref.shape[0])
+    rows = pl.ds(index, FINE, stride=pitch(table_ref.shape[0]))
     data = jnp.concatenate([ref[rows, :] for ref in time_refs], axis=1).astype(jnp.bfloat16)
     data = jnp.concatenate([data, data], axis=0)
     data = jnp.dot(table_ref[index], data, preferred_element_type=jnp.float32)
-    for k, ref in enumerate(freq_refs):
-        ref[index] = data[:, k * LANES : (k + 1) * LANES]
-
-
-def back(table_ref, freq_refs, time_refs, index):
-    rows = pl.ds(index, FINE, stride=table_ref.shape[0])
+    return [(ref, (index,), data[:, k * LANES : (k + 1) * LANES]) for k, ref in enumerate(freq_refs)]
+
+
+def back(table_ref, freq_refs, time_refs, finish, index):
+    rows = pl.ds(index, FINE, stride=pitch(table_ref.shape[0]))
     data = jnp.concatenate([ref[index] for ref in freq_refs], axis=1)
     high = data.astype(jnp.bfloat16)
     low = (data - high.astype(jnp.float32)).astype(jnp.bfloat16)
@@ -117,8 +151,7 @@
     table = jnp.concatenate([table, table[:, : 2 * FINE]], axis=1)
     data = jnp.concatenate([high, high, low], axis=0)
     data = jnp.dot(table, data, preferred_element_type=jnp.float32)
-    for k, ref in enumerate(time_refs):
-        ref[rows, :] = data[:, k * LANES : (k + 1) * LANES]
+    return [(ref, (rows,), part) for ref, part in zip(time_refs, finish(data[:, :LANES], data[:, LANES:]))]
 
 
 def rows_of(index):
@@ -131,59 +164,54 @@
     return [(freq_ref[c, real, :], freq_ref[c, imag, :]) for c in range(freq_ref.shape[0])]
 
 
-def store(freq_ref, index, data):
+def stores(freq_ref, index, data):
     real, imag = rows_of(index)
-    for c, (dr, di) in enumerate(data):
-        freq_ref[c, real, :] = dr
-        freq_ref[c, imag, :] = di
+    return [(freq_ref, (c, rows), part) for c, pair in enumerate(data) for rows, part in zip((real, imag), pair)]
 
 
 def spectrum(freq_ref, index):
-    store(freq_ref, index, fourier(load(freq_ref, index), -1))
+    return stores(freq_ref, index, fourier(load(freq_ref, index), -1))
 
 
 def correlate(freq_ref, cot_ref, index):
-    real, imag = rows_of(index)
-    products = []
-    for c, (br, bi) in enumerate(fourier(load(freq_ref, index), -1)):
-        cr, ci = cot_ref[c, real, :], cot_ref[c, imag, :]
-        products.append((br * cr + bi * ci, br * ci - bi * cr))
-    store(freq_ref, index, fourier(products, 1))
-
-
-def each(count, step, unroll):
+    data, cot = load(freq_ref, index), load(cot_ref, index)
+    products = [
+        (br * cr + bi * ci, br * ci - bi * cr) for (br, bi), (cr, ci) in zip(fourier(data, -1), cot)
+    ]
+    return stores(freq_ref, index, fourier(products, 1))
+
+
+def each(count, steps, unroll):
     def body(index, carry):
-        step(index)
+        for ref, where, value in [item for step in steps for item in step(index)]:
+            ref[where] = value
         return carry
 
     lax.fori_loop(0, count, body, 0, unroll=min(unroll, count))
 
 
-def gradients(forward_ref, inverse_ref, times, freqs, fetch):
+def gradients(forward_ref, inverse_ref, times, freqs, fetch, finish):
     sig_time, cot_time, fil_time = times
     sig_freq, cot_freq, fil_freq = freqs
-    coarse = forward_ref.shape[0]
+    coarse, slabs = forward_ref.shape[0], FINE // SLAB
 
     def beside(matrix, vector, unroll):
-        def step(index):
-            matrix(index)
-            if coarse * SLAB == FINE:
-                vector(index)
-            else:
-                pl.when(index < FINE // SLAB)(lambda: vector(index))
-
-        each(coarse, step, unroll)
-
-    each(coarse, lambda i: onward(forward_ref, (cot_time,), (cot_freq,), i), UNROLL[0])
+        if coarse == slabs:
+            each(coarse, (vector, matrix), unroll)
+        else:
+            each(coarse, (matrix,), unroll)
+            each(slabs, (vector,), unroll)
+
+    each(coarse, (lambda i: onward(forward_ref, (cot_time,), (cot_freq,), i),), UNROLL[0])
     beside(
         lambda i: onward(forward_ref, (fil_time, sig_time), (fil_freq, sig_freq), i),
         lambda i: spectrum(cot_freq, i),
         UNROLL[1],
     )
-    each(FINE // SLAB, lambda i: correlate(fil_freq, cot_freq, i), UNROLL[2])
-    each(FINE // SLAB, lambda i: correlate(sig_freq, cot_freq, i), UNROLL[3])
+    each(slabs, (lambda i: correlate(fil_freq, cot_freq, i),), UNROLL[2])
+    each(slabs, (lambda i: correlate(sig_freq, cot_freq, i),), UNROLL[3])
     fetch.wait()
-    each(coarse, lambda i: back(inverse_ref, (sig_freq, fil_freq), (sig_time, fil_time), i), UNROLL[4])
+    each(coarse, (lambda i: back(inverse_ref, (fil_freq, sig_freq), times[:2], finish, i),), UNROLL[4])
 
 
 UNROLL = (16, 16, 4, 4, 16)
@@ -193,46 +221,70 @@
     times, freqs = scratch[:3], scratch[3:]
     _, places, depth, _ = in_ref.shape
     rows = out_ref.shape[2]
-    quarter = rows // 4
     fetch = pltpu.make_async_copy(inverse_hbm, inverse_ref, arrived)
     fetch.start()
 
+    coarse = forward_ref.shape[0]
+    groups = rows // coarse
+
+    def span(place, group):
+        return pl.ds(pl.multiple_of((place * groups + group) * pitch(coarse), 8), coarse)
+
     def unfold(place):
-        start = pl.multiple_of(place * rows, rows)
-        first, second = (in_ref[k, place, :rows, :].astype(jnp.float32) for k in range(2))
-        times[0][pl.ds(start, rows), :] = merge(first, second)
-        times[1][pl.ds(start, rows), :] = merge_right(first, second)
+        first, second = in_ref[0, place, :rows, :], in_ref[1, place, :rows, :]
+        folds = [in_ref[k, place, rows:, :] for k in range(2)]
+        fil = jnp.concatenate([part for fold in folds for part in (merge(fold, fold), merge_right(fold, fold))], axis=0)
+        for ref, data in zip(times, (merge(first, second), merge_right(first, second), fil)):
+            data = data.astype(jnp.float32)
+            for group in range(groups):
+                ref[span(place, group), :] = data[group * coarse : (group + 1) * coarse]
+        return ()
+
+    def finish(sig, fil):
+        left = left_lanes(sig.shape)
+        fil = fil + pltpu.roll(fil, HALF, 1)
+        return jnp.where(left, sig, fil), jnp.where(left, pltpu.roll(sig, HALF, 1), fil)
+
+    def fold(place):
         for k in range(2):
-            fold = in_ref[k, place, rows:, :].astype(jnp.float32)
-            times[2][pl.ds(start + 2 * k * quarter, quarter), :] = merge(fold, fold)
-            times[2][pl.ds(start + (2 * k + 1) * quarter, quarter), :] = merge_right(fold, fold)
-
-    each(places, unfold, 16)
-    gradients(forward_ref, inverse_ref, times, freqs, fetch)
-
-    def fold(place):
-        span = pl.ds(pl.multiple_of(place * rows, rows), rows)
-        sig, fil = times[2][span, :], times[0][span, :]
-        fil = fil + pltpu.roll(fil, HALF, 1)
-        left = left_lanes(sig.shape)
-        out_ref[0, place] = jnp.where(left, sig, fil).astype(jnp.bfloat16)
-        out_ref[1, place] = jnp.where(left, pltpu.roll(sig, HALF, 1), fil).astype(jnp.bfloat16)
-
-    each(places, fold, 16)
+            data = jnp.concatenate([times[k][span(place, group), :] for group in range(groups)], axis=0)
+            out_ref[k, place] = data.astype(jnp.bfloat16)
+        return ()
+
+    each(places, (unfold,), 16)
+    gradients(forward_ref, inverse_ref, times, freqs, fetch, finish)
+    each(places, (fold,), 16)
 
 
 def plain_core(groups, forward_ref, inverse_hbm, in_ref, out_ref, inverse_ref, arrived, *scratch):
     times, freqs = scratch[:3], scratch[3:]
     fetch = pltpu.make_async_copy(inverse_hbm, inverse_ref, arrived)
     fetch.start()
-    for k in range(3):
-        times[k][...] = in_ref[k].astype(jnp.float32)
-    gradients(forward_ref, inverse_ref, times, freqs, fetch)
-    fil, step = times[0][...], LANES // groups
-    while step < LANES:
-        fil, step = fil + pltpu.roll(fil, step, 1), 2 * step
-    out_ref[0] = times[2][...].astype(jnp.bfloat16)
-    out_ref[1] = fil.astype(jnp.bfloat16)
+    coarse = forward_ref.shape[0]
+
+    def spans(group):
+        return (
+            pl.ds(pl.multiple_of(group * pitch(coarse), 8), coarse),
+            pl.ds(pl.multiple_of(group * coarse, coarse), coarse),
+        )
+
+    def unfold(group):
+        to, span = spans(group)
+        return [(times[k], (to,), in_ref[k, span, :].astype(jnp.float32)) for k in range(3)]
+
+    def finish(sig, fil):
+        step = LANES // groups
+        while step < LANES:
+            fil, step = fil + pltpu.roll(fil, step, 1), 2 * step
+        return sig, fil
+
+    def fold(group):
+        to, span = spans(group)
+        return [(out_ref, (k, span), times[k][to, :].astype(jnp.bfloat16)) for k in range(2)]
+
+    each(FINE, (unfold,), 8)
+    gradients(forward_ref, inverse_ref, times, freqs, fetch, finish)
+    each(FINE, (fold,), 8)
 
 
 def core(kernel, message, out_shape, total):
@@ -245,9 +297,9 @@
         out_specs=vmem,
         out_shape=pltpu.VMEM(out_shape, jnp.bfloat16),
         scratch_shapes=[pltpu.VMEM(inverse.shape, jnp.bfloat16), pltpu.SemaphoreType.DMA]
-        + [pltpu.VMEM((total, LANES), jnp.float32)] * 3
+        + [pltpu.VMEM((FINE * pitch(coarse), LANES), jnp.float32)] * 3
         + [pltpu.VMEM((coarse, 2 * FINE, LANES), jnp.float32)] * 3,
-        compiler_params=pltpu.CompilerParams(vmem_limit_bytes=total * 11 * 2**10),
+        compiler_params=pltpu.CompilerParams(vmem_limit_bytes=total * 12 * 2**10),
         name="gradients",
     )(jnp.asarray(forward), jnp.asarray(inverse), pltpu.with_memory_space_constraint(message, pltpu.VMEM))
 
@@ -260,15 +312,18 @@
     rows, columns = signal.shape
     places = lax.axis_size("cp")
     depth = rows + rows // 4
-    steps = 2
-    block = places // steps
-    column = pl.BlockSpec((rows, columns // steps), lambda j: (0, j))
+    hbm, vmem = pl.BlockSpec(memory_space=pltpu.HBM), pl.BlockSpec(memory_space=pltpu.VMEM)
     message = pl.pallas_call(
         pack_kernel,
-        grid=(steps,),
-        in_specs=[pl.BlockSpec(memory_space=pltpu.SMEM), column, column, column],
-        out_specs=pl.BlockSpec((2, block, depth, LANES), lambda j: (0, j, 0, 0)),
+        in_specs=[pl.BlockSpec(memory_space=pltpu.SMEM), hbm, hbm, hbm],
+        out_specs=vmem,
         out_shape=pltpu.VMEM((2, places, depth, LANES), jnp.bfloat16),
+        scratch_shapes=[
+            pltpu.VMEM((rows, columns), jnp.bfloat16),
+            pltpu.VMEM((rows, columns), jnp.bfloat16),
+            pltpu.VMEM((rows // 2, columns), jnp.bfloat16),
+            pltpu.SemaphoreType.DMA((3, IN_CHUNKS)),
+        ],
         name="pack",
     )(lax.axis_index("tp").reshape(1), signal, cotangent, long_filter)
     message = exchange(message.reshape(2 * places, depth, LANES)).reshape(2, places, depth, LANES)
@@ -276,10 +331,10 @@
     message = exchange(message.reshape(2 * places, rows, LANES)).reshape(2, places, rows, LANES)
     return pl.pallas_call(
         unpack_kernel,
-        grid=(steps,),
-        in_specs=[pl.BlockSpec((2, block, rows, LANES), lambda j: (0, j, 0, 0))],
-        out_specs=[column, column],
+        in_specs=[vmem],
+        out_specs=[hbm, hbm],
         out_shape=[jax.ShapeDtypeStruct((rows, columns), jnp.bfloat16)] * 2,
+        scratch_shapes=[pltpu.VMEM((rows, columns), jnp.bfloat16)] * 2 + [pltpu.SemaphoreType.DMA((2, OUT_CHUNKS))],
         name="unpack",
     )(pltpu.with_memory_space_constraint(message, pltpu.VMEM))
 

time: 80.2 us -> 79.1 us (0.986)
  Pallas kernels: 10 us -> 8.9 us
    pallas_call x1, Pallas kernels: 6.84 us -> 6 us  [core(): pl.pallas_call(kernel, in_specs=[vmem, pl.BlockSpec(memory_space=pltpu.HB...]
where the time goes in v4:
time: 79.1 us; the launch traced here: 78.9 us
  blocking collectives  69.3 us (88%)
  Pallas kernels  8.9 us (11%)
    all_to_all x2, blocking collectives, exchange(): lax.all_to_all(message, both, split_axis=0, concat_axis=0, tiled=True)  69.3 us
    pallas_call x1, Pallas kernels, core(): pl.pallas_call(kernel, in_specs=[vmem, pl.BlockSpec(memory_space=pltpu.HB...  6 us
    pallas_call x1, Pallas kernels, packed_body(): pl.pallas_call(pack_kernel, in_specs=[pl.BlockSpec(memory_space=pltpu.SME...  1.75 us

profile of v4, /device:TPU:0, one launch (start us, length us, event | category | flops | bytes accessed | tf_op | source)
XLA Modules:
  0.0 78.9 jit_solution(18084309417740917869)
XLA Ops:
  0.6 0.0 copy-start
  0.6 1.7 %pack.1 = bf16[2,16,160,128]{3,2,1,0:T(8,128)(2,1)S(1)} custom-call(s32[1]{0:T(128)} %bitcast.part_ref, bf16[128,2048]{1,0:T(8,128)(2,1)} %sig_hbm.1, bf16[128,2048]{1,0:T(8,128)(2,1)} %cot_hbm.1, bf16[128,2048]{1,0:T(8,128)(2,1)} %fil_hbm.1), custom_call_target="tpu_custom_call" | custom-call | tf_op jit(solution)/shard_map/pack/pallas_call | solution.py:316
  2.4 0.0 copy-start.1
  2.4 39.9 %all_to_all.10 = bf16[32,160,128]{2,1,0:T(8,128)(2,1)S(1)} all-to-all(bf16[32,160,128]{2,1,0:T(8,128)(2,1)S(1)} %bitcast.5), channel_id=1, replica_groups=mesh['tp'=2,'cp'=16] {'tp','cp'}, dimensions={0} | all-to-all | bytes 2621440 | tf_op jit(solution)/shard_map/all_to_all | solution.py:308
  42.3 0.0 copy-done
  42.3 0.0 copy-done.1
  42.3 6.0 %gradients.1 = bf16[2,16,128,128]{3,2,1,0:T(8,128)(2,1)S(1)} custom-call(bf16[16,256,256]{2,1,0:T(8,128)(2,1)S(1)} %copy-done.1, bf16[16,128,512]{2,1,0:T(8,128)(2,1)S(1)} %copy-done, bf16[2,16,160,128]{3,2,1,0:T(8,128)(2,1)S(1)} %bitcast.6), custom_call_target="tpu_custom_call" | custom-call | tf_op jit(solution)/shard_map/gradients/pallas_call | solution.py:294
  48.3 29.4 %all_to_all.11 = bf16[32,128,128]{2,1,0:T(8,128)(2,1)S(1)} all-to-all(bf16[32,128,128]{2,1,0:T(8,128)(2,1)S(1)} %bitcast.7), channel_id=1, replica_groups=mesh['tp'=2,'cp'=16] {'tp','cp'}, dimensions={0} | all-to-all | bytes 2097152 | tf_op jit(solution)/shard_map/all_to_all | solution.py:308
  77.8 1.2 %unpack.1 = (bf16[128,2048]{1,0:T(8,128)(2,1)}, bf16[128,2048]{1,0:T(8,128)(2,1)}) custom-call(bf16[2,16,128,128]{3,2,1,0:T(8,128)(2,1)S(1)} %bitcast.8), custom_call_target="tpu_custom_call" | custom-call | tf_op jit(solution)/shard_map/unpack/pallas_call | solution.py:332
Async XLA Ops:
  0.6 41.7 %copy-start = (bf16[16,128,512]{2,1,0:T(8,128)(2,1)S(1)}, bf16[16,128,512]{2,1,0:T(8,128)(2,1)}, u32[]{:S(2)}) copy-start(bf16[16,128,512]{2,1,0:T(8,128)(2,1)} %constant.11.clone.inverse_hbm) | copy-start | bytes 6291460
  2.4 39.9 %copy-start.1 = (bf16[16,256,256]{2,1,0:T(8,128)(2,1)S(1)}, bf16[16,256,256]{2,1,0:T(8,128)(2,1)}, u32[]{:S(2)}) copy-start(bf16[16,256,256]{2,1,0:T(8,128)(2,1)} %constant.10.clone.forward_ref) | copy-start | bytes 6291460

commit v5 on v4

--- a/solution.py
+++ b/solution.py
@@ -14,6 +14,7 @@
 FINE = 128
 HALF = LANES // 2
 SLAB = 8
+UNROLL = 16
 IN_CHUNKS = 2
 OUT_CHUNKS = 4
 both = ("tp", "cp")
@@ -181,13 +182,13 @@
     return stores(freq_ref, index, fourier(products, 1))
 
 
-def each(count, steps, unroll):
+def each(count, steps):
     def body(index, carry):
         for ref, where, value in [item for step in steps for item in step(index)]:
             ref[where] = value
         return carry
 
-    lax.fori_loop(0, count, body, 0, unroll=min(unroll, count))
+    lax.fori_loop(0, count, body, 0, unroll=min(UNROLL, count))
 
 
 def gradients(forward_ref, inverse_ref, times, freqs, fetch, finish):
@@ -195,26 +196,13 @@
     sig_freq, cot_freq, fil_freq = freqs
     coarse, slabs = forward_ref.shape[0], FINE // SLAB
 
-    def beside(matrix, vector, unroll):
-        if coarse == slabs:
-            each(coarse, (vector, matrix), unroll)
-        else:
-            each(coarse, (matrix,), unroll)
-            each(slabs, (vector,), unroll)
-
-    each(coarse, (lambda i: onward(forward_ref, (cot_time,), (cot_freq,), i),), UNROLL[0])
-    beside(
-        lambda i: onward(forward_ref, (fil_time, sig_time), (fil_freq, sig_freq), i),
-        lambda i: spectrum(cot_freq, i),
-        UNROLL[1],
-    )
-    each(slabs, (lambda i: correlate(fil_freq, cot_freq, i),), UNROLL[2])
-    each(slabs, (lambda i: correlate(sig_freq, cot_freq, i),), UNROLL[3])
+    each(coarse, (lambda i: onward(forward_ref, (cot_time, fil_time), (cot_freq, fil_freq), i),))
+    each(coarse, (lambda i: onward(forward_ref, (sig_time,), (sig_freq,), i),))
+    each(slabs, (lambda i: spectrum(cot_freq, i),))
+    each(slabs, (lambda i: correlate(fil_freq, cot_freq, i),))
+    each(slabs, (lambda i: correlate(sig_freq, cot_freq, i),))
     fetch.wait()
-    each(coarse, (lambda i: back(inverse_ref, (fil_freq, sig_freq), times[:2], finish, i),), UNROLL[4])
-
-
-UNROLL = (16, 16, 4, 4, 16)
+    each(coarse, (lambda i: back(inverse_ref, (fil_freq, sig_freq), times[:2], finish, i),))
 
 
 def packed_core(forward_ref, inverse_hbm, in_ref, out_ref, inverse_ref, arrived, *scratch):
@@ -251,9 +239,9 @@
             out_ref[k, place] = data.astype(jnp.bfloat16)
         return ()
 
-    each(places, (unfold,), 16)
+    each(places, (unfold,))
     gradients(forward_ref, inverse_ref, times, freqs, fetch, finish)
-    each(places, (fold,), 16)
+    each(places, (fold,))
 
 
 def plain_core(groups, forward_ref, inverse_hbm, in_ref, out_ref, inverse_ref, arrived, *scratch):
@@ -282,9 +270,9 @@
         to, span = spans(group)
         return [(out_ref, (k, span), times[k][to, :].astype(jnp.bfloat16)) for k in range(2)]
 
-    each(FINE, (unfold,), 8)
+    each(FINE, (unfold,))
     gradients(forward_ref, inverse_ref, times, freqs, fetch, finish)
-    each(FINE, (fold,), 8)
+    each(FINE, (fold,))
 
 
 def core(kernel, message, out_shape, total):

time: 79.1 us -> 78.6 us (level)
  no operation moved by 1% of the time
where the time goes in v5:
time: 78.6 us; the launch traced here: 78.4 us
  blocking collectives  69.3 us (88%)
  Pallas kernels  8.37 us (11%)
    all_to_all x2, blocking collectives, exchange(): lax.all_to_all(message, both, split_axis=0, concat_axis=0, tiled=True)  69.3 us
    pallas_call x1, Pallas kernels, core(): pl.pallas_call(kernel, in_specs=[vmem, pl.BlockSpec(memory_space=pltpu.HB...  5.46 us
    pallas_call x1, Pallas kernels, packed_body(): pl.pallas_call(pack_kernel, in_specs=[pl.BlockSpec(memory_space=pltpu.SME...  1.75 us

profile of v5, /device:TPU:0, one launch (start us, length us, event | category | flops | bytes accessed | tf_op | source)
XLA Modules:
  0.0 78.4 jit_solution(7859818859077372724)
XLA Ops:
  0.6 0.0 copy-start
  0.6 1.7 %pack.1 = bf16[2,16,160,128]{3,2,1,0:T(8,128)(2,1)S(1)} custom-call(s32[1]{0:T(128)} %bitcast.part_ref, bf16[128,2048]{1,0:T(8,128)(2,1)} %sig_hbm.1, bf16[128,2048]{1,0:T(8,128)(2,1)} %cot_hbm.1, bf16[128,2048]{1,0:T(8,128)(2,1)} %fil_hbm.1), custom_call_target="tpu_custom_call" | custom-call | tf_op jit(solution)/shard_map/pack/pallas_call | solution.py:304
  2.4 0.0 copy-start.1
  2.4 39.9 %all_to_all.10 = bf16[32,160,128]{2,1,0:T(8,128)(2,1)S(1)} all-to-all(bf16[32,160,128]{2,1,0:T(8,128)(2,1)S(1)} %bitcast.5), channel_id=1, replica_groups=mesh['tp'=2,'cp'=16] {'tp','cp'}, dimensions={0} | all-to-all | bytes 2621440 | tf_op jit(solution)/shard_map/all_to_all | solution.py:296
  42.3 0.0 copy-done
  42.3 0.0 copy-done.1
  42.3 5.5 %gradients.1 = bf16[2,16,128,128]{3,2,1,0:T(8,128)(2,1)S(1)} custom-call(bf16[16,256,256]{2,1,0:T(8,128)(2,1)S(1)} %copy-done.1, bf16[16,128,512]{2,1,0:T(8,128)(2,1)S(1)} %copy-done, bf16[2,16,160,128]{3,2,1,0:T(8,128)(2,1)S(1)} %bitcast.6), custom_call_target="tpu_custom_call" | custom-call | tf_op jit(solution)/shard_map/gradients/pallas_call | solution.py:282
  47.8 29.4 %all_to_all.11 = bf16[32,128,128]{2,1,0:T(8,128)(2,1)S(1)} all-to-all(bf16[32,128,128]{2,1,0:T(8,128)(2,1)S(1)} %bitcast.7), channel_id=1, replica_groups=mesh['tp'=2,'cp'=16] {'tp','cp'}, dimensions={0} | all-to-all | bytes 2097152 | tf_op jit(solution)/shard_map/all_to_all | solution.py:296
  77.2 1.2 %unpack.1 = (bf16[128,2048]{1,0:T(8,128)(2,1)}, bf16[128,2048]{1,0:T(8,128)(2,1)}) custom-call(bf16[2,16,128,128]{3,2,1,0:T(8,128)(2,1)S(1)} %bitcast.8), custom_call_target="tpu_custom_call" | custom-call | tf_op jit(solution)/shard_map/unpack/pallas_call | solution.py:320
Async XLA Ops:
  0.6 41.7 %copy-start = (bf16[16,128,512]{2,1,0:T(8,128)(2,1)S(1)}, bf16[16,128,512]{2,1,0:T(8,128)(2,1)}, u32[]{:S(2)}) copy-start(bf16[16,128,512]{2,1,0:T(8,128)(2,1)} %constant.11.clone.inverse_hbm) | copy-start | bytes 6291460
  2.4 39.9 %copy-start.1 = (bf16[16,256,256]{2,1,0:T(8,128)(2,1)S(1)}, bf16[16,256,256]{2,1,0:T(8,128)(2,1)}, u32[]{:S(2)}) copy-start(bf16[16,256,256]{2,1,0:T(8,128)(2,1)} %constant.10.clone.forward_ref) | copy-start | bytes 6291460

commit v6 on v5

--- a/solution.py
+++ b/solution.py
@@ -285,7 +285,7 @@
         out_specs=vmem,
         out_shape=pltpu.VMEM(out_shape, jnp.bfloat16),
         scratch_shapes=[pltpu.VMEM(inverse.shape, jnp.bfloat16), pltpu.SemaphoreType.DMA]
-        + [pltpu.VMEM((FINE * pitch(coarse), LANES), jnp.float32)] * 3
+        + [pltpu.VMEM(((FINE + 1) * pitch(coarse), LANES), jnp.float32)] * 3
         + [pltpu.VMEM((coarse, 2 * FINE, LANES), jnp.float32)] * 3,
         compiler_params=pltpu.CompilerParams(vmem_limit_bytes=total * 12 * 2**10),
         name="gradients",

time: 78.6 us -> 78.6 us (level)
  no operation moved by 1% of the time
where the time goes in v6:
time: 78.6 us; the launch traced here: 78.4 us
  blocking collectives  69.3 us (88%)
  Pallas kernels  8.37 us (11%)
    all_to_all x2, blocking collectives, exchange(): lax.all_to_all(message, both, split_axis=0, concat_axis=0, tiled=True)  69.3 us
    pallas_call x1, Pallas kernels, core(): pl.pallas_call(kernel, in_specs=[vmem, pl.BlockSpec(memory_space=pltpu.HB...  5.47 us
    pallas_call x1, Pallas kernels, packed_body(): pl.pallas_call(pack_kernel, in_specs=[pl.BlockSpec(memory_space=pltpu.SME...  1.75 us

profile of v6, /device:TPU:0, one launch (start us, length us, event | category | flops | bytes accessed | tf_op | source)
XLA Modules:
  0.0 78.4 jit_solution(1398503588710238390)
XLA Ops:
  0.6 0.0 copy-start
  0.6 1.7 %pack.1 = bf16[2,16,160,128]{3,2,1,0:T(8,128)(2,1)S(1)} custom-call(s32[1]{0:T(128)} %bitcast.part_ref, bf16[128,2048]{1,0:T(8,128)(2,1)} %sig_hbm.1, bf16[128,2048]{1,0:T(8,128)(2,1)} %cot_hbm.1, bf16[128,2048]{1,0:T(8,128)(2,1)} %fil_hbm.1), custom_call_target="tpu_custom_call" | custom-call | tf_op jit(solution)/shard_map/pack/pallas_call | solution.py:304
  2.4 0.0 copy-start.1
  2.4 39.9 %all_to_all.10 = bf16[32,160,128]{2,1,0:T(8,128)(2,1)S(1)} all-to-all(bf16[32,160,128]{2,1,0:T(8,128)(2,1)S(1)} %bitcast.5), channel_id=1, replica_groups=mesh['tp'=2,'cp'=16] {'tp','cp'}, dimensions={0} | all-to-all | bytes 2621440 | tf_op jit(solution)/shard_map/all_to_all | solution.py:296
  42.3 0.0 copy-done
  42.3 0.0 copy-done.1
  42.3 5.5 %gradients.1 = bf16[2,16,128,128]{3,2,1,0:T(8,128)(2,1)S(1)} custom-call(bf16[16,256,256]{2,1,0:T(8,128)(2,1)S(1)} %copy-done.1, bf16[16,128,512]{2,1,0:T(8,128)(2,1)S(1)} %copy-done, bf16[2,16,160,128]{3,2,1,0:T(8,128)(2,1)S(1)} %bitcast.6), custom_call_target="tpu_custom_call" | custom-call | tf_op jit(solution)/shard_map/gradients/pallas_call | solution.py:282
  47.8 29.4 %all_to_all.11 = bf16[32,128,128]{2,1,0:T(8,128)(2,1)S(1)} all-to-all(bf16[32,128,128]{2,1,0:T(8,128)(2,1)S(1)} %bitcast.7), channel_id=1, replica_groups=mesh['tp'=2,'cp'=16] {'tp','cp'}, dimensions={0} | all-to-all | bytes 2097152 | tf_op jit(solution)/shard_map/all_to_all | solution.py:296
  77.2 1.2 %unpack.1 = (bf16[128,2048]{1,0:T(8,128)(2,1)}, bf16[128,2048]{1,0:T(8,128)(2,1)}) custom-call(bf16[2,16,128,128]{3,2,1,0:T(8,128)(2,1)S(1)} %bitcast.8), custom_call_target="tpu_custom_call" | custom-call | tf_op jit(solution)/shard_map/unpack/pallas_call | solution.py:320
Async XLA Ops:
  0.6 41.7 %copy-start = (bf16[16,128,512]{2,1,0:T(8,128)(2,1)S(1)}, bf16[16,128,512]{2,1,0:T(8,128)(2,1)}, u32[]{:S(2)}) copy-start(bf16[16,128,512]{2,1,0:T(8,128)(2,1)} %constant.11.clone.inverse_hbm) | copy-start | bytes 6291460
  2.4 39.9 %copy-start.1 = (bf16[16,256,256]{2,1,0:T(8,128)(2,1)S(1)}, bf16[16,256,256]{2,1,0:T(8,128)(2,1)}, u32[]{:S(2)}) copy-start(bf16[16,256,256]{2,1,0:T(8,128)(2,1)} %constant.10.clone.forward_ref) | copy-start | bytes 6291460

commit v7 on v6

--- a/solution.py
+++ b/solution.py
@@ -143,12 +143,11 @@
     return [(ref, (index,), data[:, k * LANES : (k + 1) * LANES]) for k, ref in enumerate(freq_refs)]
 
 
-def back(table_ref, freq_refs, time_refs, finish, index):
-    rows = pl.ds(index, FINE, stride=pitch(table_ref.shape[0]))
+def back(table, coarse, freq_refs, time_refs, finish, index):
+    rows = pl.ds(index, FINE, stride=pitch(coarse))
     data = jnp.concatenate([ref[index] for ref in freq_refs], axis=1)
     high = data.astype(jnp.bfloat16)
     low = (data - high.astype(jnp.float32)).astype(jnp.bfloat16)
-    table = table_ref[index]
     table = jnp.concatenate([table, table[:, : 2 * FINE]], axis=1)
     data = jnp.concatenate([high, high, low], axis=0)
     data = jnp.dot(table, data, preferred_element_type=jnp.float32)
@@ -191,7 +190,7 @@
     lax.fori_loop(0, count, body, 0, unroll=min(UNROLL, count))
 
 
-def gradients(forward_ref, inverse_ref, times, freqs, fetch, finish):
+def gradients(forward_ref, inverse_ref, first_ref, times, freqs, fetch, finish):
     sig_time, cot_time, fil_time = times
     sig_freq, cot_freq, fil_freq = freqs
     coarse, slabs = forward_ref.shape[0], FINE // SLAB
@@ -202,14 +201,17 @@
     each(slabs, (lambda i: correlate(fil_freq, cot_freq, i),))
     each(slabs, (lambda i: correlate(sig_freq, cot_freq, i),))
     fetch.wait()
-    each(coarse, (lambda i: back(inverse_ref, (fil_freq, sig_freq), times[:2], finish, i),))
-
-
-def packed_core(forward_ref, inverse_hbm, in_ref, out_ref, inverse_ref, arrived, *scratch):
+    for index in range(coarse):
+        table = inverse_ref[index] if index else first_ref[...]
+        for ref, where, value in back(table, coarse, (fil_freq, sig_freq), times[:2], finish, index):
+            ref[where] = value
+
+
+def packed_core(forward_ref, inverse_ref, in_ref, out_ref, first_ref, arrived, *scratch):
     times, freqs = scratch[:3], scratch[3:]
     _, places, depth, _ = in_ref.shape
     rows = out_ref.shape[2]
-    fetch = pltpu.make_async_copy(inverse_hbm, inverse_ref, arrived)
+    fetch = pltpu.make_async_copy(inverse_ref.at[0], first_ref, arrived)
     fetch.start()
 
     coarse = forward_ref.shape[0]
@@ -240,13 +242,13 @@
         return ()
 
     each(places, (unfold,))
-    gradients(forward_ref, inverse_ref, times, freqs, fetch, finish)
+    gradients(forward_ref, inverse_ref, first_ref, times, freqs, fetch, finish)
     each(places, (fold,))
 
 
-def plain_core(groups, forward_ref, inverse_hbm, in_ref, out_ref, inverse_ref, arrived, *scratch):
+def plain_core(groups, forward_ref, inverse_ref, in_ref, out_ref, first_ref, arrived, *scratch):
     times, freqs = scratch[:3], scratch[3:]
-    fetch = pltpu.make_async_copy(inverse_hbm, inverse_ref, arrived)
+    fetch = pltpu.make_async_copy(inverse_ref.at[0], first_ref, arrived)
     fetch.start()
     coarse = forward_ref.shape[0]
 
@@ -271,7 +273,7 @@
         return [(out_ref, (k, span), times[k][to, :].astype(jnp.bfloat16)) for k in range(2)]
 
     each(FINE, (unfold,))
-    gradients(forward_ref, inverse_ref, times, freqs, fetch, finish)
+    gradients(forward_ref, inverse_ref, first_ref, times, freqs, fetch, finish)
     each(FINE, (fold,))
 
 
@@ -281,10 +283,10 @@
     vmem = pl.BlockSpec(memory_space=pltpu.VMEM)
     return pl.pallas_call(
         kernel,
-        in_specs=[vmem, pl.BlockSpec(memory_space=pltpu.HBM), vmem],
+        in_specs=[vmem, vmem, vmem],
         out_specs=vmem,
         out_shape=pltpu.VMEM(out_shape, jnp.bfloat16),
-        scratch_shapes=[pltpu.VMEM(inverse.shape, jnp.bfloat16), pltpu.SemaphoreType.DMA]
+        scratch_shapes=[pltpu.VMEM(inverse.shape[1:], jnp.bfloat16), pltpu.SemaphoreType.DMA]
         + [pltpu.VMEM(((FINE + 1) * pitch(coarse), LANES), jnp.float32)] * 3
         + [pltpu.VMEM((coarse, 2 * FINE, LANES), jnp.float32)] * 3,
         compiler_params=pltpu.CompilerParams(vmem_limit_bytes=total * 12 * 2**10),

time: 78.6 us -> 78.6 us (level)
  no operation moved by 1% of the time
where the time goes in v7:
time: 78.6 us; the launch traced here: 78.4 us
  blocking collectives  69.4 us (88%)
  Pallas kernels  8.38 us (11%)
    all_to_all x2, blocking collectives, exchange(): lax.all_to_all(message, both, split_axis=0, concat_axis=0, tiled=True)  69.4 us
    pallas_call x1, Pallas kernels, core(): pl.pallas_call(kernel, in_specs=[vmem, vmem, vmem], out_specs=vmem, out_s...  5.47 us
    pallas_call x1, Pallas kernels, packed_body(): pl.pallas_call(pack_kernel, in_specs=[pl.BlockSpec(memory_space=pltpu.SME...  1.75 us

profile of v7, /device:TPU:0, one launch (start us, length us, event | category | flops | bytes accessed | tf_op | source)
XLA Modules:
  0.0 78.4 jit_solution(7649242666997147562)
XLA Ops:
  0.6 0.0 copy-start
  0.6 1.7 %pack.1 = bf16[2,16,160,128]{3,2,1,0:T(8,128)(2,1)S(1)} custom-call(s32[1]{0:T(128)} %bitcast.part_ref, bf16[128,2048]{1,0:T(8,128)(2,1)} %sig_hbm.1, bf16[128,2048]{1,0:T(8,128)(2,1)} %cot_hbm.1, bf16[128,2048]{1,0:T(8,128)(2,1)} %fil_hbm.1), custom_call_target="tpu_custom_call" | custom-call | tf_op jit(solution)/shard_map/pack/pallas_call | solution.py:306
  2.4 0.0 copy-start.1
  2.4 39.9 %all_to_all.10 = bf16[32,160,128]{2,1,0:T(8,128)(2,1)S(1)} all-to-all(bf16[32,160,128]{2,1,0:T(8,128)(2,1)S(1)} %bitcast.5), channel_id=1, replica_groups=mesh['tp'=2,'cp'=16] {'tp','cp'}, dimensions={0} | all-to-all | bytes 2621440 | tf_op jit(solution)/shard_map/all_to_all | solution.py:298
  42.3 0.0 copy-done
  42.3 0.0 copy-done.1
  42.3 5.5 %gradients.1 = bf16[2,16,128,128]{3,2,1,0:T(8,128)(2,1)S(1)} custom-call(bf16[16,256,256]{2,1,0:T(8,128)(2,1)S(1)} %copy-done.1, bf16[16,128,512]{2,1,0:T(8,128)(2,1)S(1)} %copy-done, bf16[2,16,160,128]{3,2,1,0:T(8,128)(2,1)S(1)} %bitcast.6), custom_call_target="tpu_custom_call" | custom-call | tf_op jit(solution)/shard_map/gradients/pallas_call | solution.py:284
  47.8 29.5 %all_to_all.11 = bf16[32,128,128]{2,1,0:T(8,128)(2,1)S(1)} all-to-all(bf16[32,128,128]{2,1,0:T(8,128)(2,1)S(1)} %bitcast.7), channel_id=1, replica_groups=mesh['tp'=2,'cp'=16] {'tp','cp'}, dimensions={0} | all-to-all | bytes 2097152 | tf_op jit(solution)/shard_map/all_to_all | solution.py:298
  77.3 1.2 %unpack.1 = (bf16[128,2048]{1,0:T(8,128)(2,1)}, bf16[128,2048]{1,0:T(8,128)(2,1)}) custom-call(bf16[2,16,128,128]{3,2,1,0:T(8,128)(2,1)S(1)} %bitcast.8), custom_call_target="tpu_custom_call" | custom-call | tf_op jit(solution)/shard_map/unpack/pallas_call | solution.py:322
Async XLA Ops:
  0.6 41.7 %copy-start = (bf16[16,128,512]{2,1,0:T(8,128)(2,1)S(1)}, bf16[16,128,512]{2,1,0:T(8,128)(2,1)}, u32[]{:S(2)}) copy-start(bf16[16,128,512]{2,1,0:T(8,128)(2,1)} %constant.11.clone.inverse_ref) | copy-start | bytes 6291460
  2.4 39.9 %copy-start.1 = (bf16[16,256,256]{2,1,0:T(8,128)(2,1)S(1)}, bf16[16,256,256]{2,1,0:T(8,128)(2,1)}, u32[]{:S(2)}) copy-start(bf16[16,256,256]{2,1,0:T(8,128)(2,1)} %constant.10.clone.forward_ref) | copy-start | bytes 6291460

commit v8 on v7

--- a/solution.py
+++ b/solution.py
@@ -231,14 +231,17 @@
         return ()
 
     def finish(sig, fil):
+        fil = fil + pltpu.roll(fil, HALF, 1)
+        return sig, fil
+
+    def fold(place):
+        sig, fil = (
+            jnp.concatenate([ref[span(place, group), :] for group in range(groups)], axis=0).astype(jnp.bfloat16)
+            for ref in times[:2]
+        )
         left = left_lanes(sig.shape)
-        fil = fil + pltpu.roll(fil, HALF, 1)
-        return jnp.where(left, sig, fil), jnp.where(left, pltpu.roll(sig, HALF, 1), fil)
-
-    def fold(place):
-        for k in range(2):
-            data = jnp.concatenate([times[k][span(place, group), :] for group in range(groups)], axis=0)
-            out_ref[k, place] = data.astype(jnp.bfloat16)
+        out_ref[0, place] = jnp.where(left, sig, fil)
+        out_ref[1, place] = jnp.where(left, pltpu.roll(sig, HALF, 1), fil)
         return ()
 
     each(places, (unfold,))

time: 78.6 us -> 78.5 us (level)
  no operation moved by 1% of the time
where the time goes in v8:
time: 78.5 us; the launch traced here: 78.4 us
  blocking collectives  69.3 us (88%)
  Pallas kernels  8.34 us (11%)
    all_to_all x2, blocking collectives, exchange(): lax.all_to_all(message, both, split_axis=0, concat_axis=0, tiled=True)  69.3 us
    pallas_call x1, Pallas kernels, core(): pl.pallas_call(kernel, in_specs=[vmem, vmem, vmem], out_specs=vmem, out_s...  5.43 us
    pallas_call x1, Pallas kernels, packed_body(): pl.pallas_call(pack_kernel, in_specs=[pl.BlockSpec(memory_space=pltpu.SME...  1.75 us

profile of v8, /device:TPU:0, one launch (start us, length us, event | category | flops | bytes accessed | tf_op | source)
XLA Modules:
  0.0 78.4 jit_solution(10579458622822067904)
XLA Ops:
  0.6 0.0 copy-start
  0.6 1.7 %pack.1 = bf16[2,16,160,128]{3,2,1,0:T(8,128)(2,1)S(1)} custom-call(s32[1]{0:T(128)} %bitcast.part_ref, bf16[128,2048]{1,0:T(8,128)(2,1)} %sig_hbm.1, bf16[128,2048]{1,0:T(8,128)(2,1)} %cot_hbm.1, bf16[128,2048]{1,0:T(8,128)(2,1)} %fil_hbm.1), custom_call_target="tpu_custom_call" | custom-call | tf_op jit(solution)/shard_map/pack/pallas_call | solution.py:309
  2.4 0.0 copy-start.1
  2.4 39.9 %all_to_all.10 = bf16[32,160,128]{2,1,0:T(8,128)(2,1)S(1)} all-to-all(bf16[32,160,128]{2,1,0:T(8,128)(2,1)S(1)} %bitcast.5), channel_id=1, replica_groups=mesh['tp'=2,'cp'=16] {'tp','cp'}, dimensions={0} | all-to-all | bytes 2621440 | tf_op jit(solution)/shard_map/all_to_all | solution.py:301
  42.3 0.0 copy-done
  42.3 0.0 copy-done.1
  42.3 5.4 %gradients.1 = bf16[2,16,128,128]{3,2,1,0:T(8,128)(2,1)S(1)} custom-call(bf16[16,256,256]{2,1,0:T(8,128)(2,1)S(1)} %copy-done.1, bf16[16,128,512]{2,1,0:T(8,128)(2,1)S(1)} %copy-done, bf16[2,16,160,128]{3,2,1,0:T(8,128)(2,1)S(1)} %bitcast.6), custom_call_target="tpu_custom_call" | custom-call | tf_op jit(solution)/shard_map/gradients/pallas_call | solution.py:287
  47.8 29.4 %all_to_all.11 = bf16[32,128,128]{2,1,0:T(8,128)(2,1)S(1)} all-to-all(bf16[32,128,128]{2,1,0:T(8,128)(2,1)S(1)} %bitcast.7), channel_id=1, replica_groups=mesh['tp'=2,'cp'=16] {'tp','cp'}, dimensions={0} | all-to-all | bytes 2097152 | tf_op jit(solution)/shard_map/all_to_all | solution.py:301
  77.2 1.2 %unpack.1 = (bf16[128,2048]{1,0:T(8,128)(2,1)}, bf16[128,2048]{1,0:T(8,128)(2,1)}) custom-call(bf16[2,16,128,128]{3,2,1,0:T(8,128)(2,1)S(1)} %bitcast.8), custom_call_target="tpu_custom_call" | custom-call | tf_op jit(solution)/shard_map/unpack/pallas_call | solution.py:325
Async XLA Ops:
  0.6 41.7 %copy-start = (bf16[16,128,512]{2,1,0:T(8,128)(2,1)S(1)}, bf16[16,128,512]{2,1,0:T(8,128)(2,1)}, u32[]{:S(2)}) copy-start(bf16[16,128,512]{2,1,0:T(8,128)(2,1)} %constant.11.clone.inverse_ref) | copy-start | bytes 6291460
  2.4 39.9 %copy-start.1 = (bf16[16,256,256]{2,1,0:T(8,128)(2,1)S(1)}, bf16[16,256,256]{2,1,0:T(8,128)(2,1)}, u32[]{:S(2)}) copy-start(bf16[16,256,256]{2,1,0:T(8,128)(2,1)} %constant.10.clone.forward_ref) | copy-start | bytes 6291460

commit v9 on v8

--- a/solution.py
+++ b/solution.py
@@ -86,19 +86,24 @@
     start = pl.multiple_of(part_ref[0] * 2 * quarter, 2 * quarter)
     chunk = columns // IN_CHUNKS
     copies = []
+    share = pltpu.make_async_copy(fil_hbm.at[pl.ds(start, 2 * quarter)], fil_ref, arrived.at[2, 0])
+    share.start()
     for c in range(IN_CHUNKS):
         lanes = pl.ds(c * chunk, chunk)
         copies.append(
             (
                 pltpu.make_async_copy(sig_hbm.at[:, lanes], sig_ref.at[:, lanes], arrived.at[0, c]),
                 pltpu.make_async_copy(cot_hbm.at[:, lanes], cot_ref.at[:, lanes], arrived.at[1, c]),
-                pltpu.make_async_copy(
-                    fil_hbm.at[pl.ds(start, 2 * quarter), lanes], fil_ref.at[:, lanes], arrived.at[2, c]
-                ),
             )
         )
         for copy in copies[c]:
             copy.start()
+    share.wait()
+    for place in range(columns // LANES):
+        lanes = pl.ds(place * LANES, LANES)
+        top, bottom = fil_ref[:quarter, lanes], fil_ref[quarter:, lanes]
+        out_ref[0, place, rows:, :] = merge(top, bottom)
+        out_ref[1, place, rows:, :] = merge_right(top, bottom)
     for c in range(IN_CHUNKS):
         for copy in copies[c]:
             copy.wait()
@@ -107,9 +112,6 @@
             sig, cot = sig_ref[:, lanes], cot_ref[:, lanes]
             out_ref[0, place, :rows, :] = merge(sig, cot)
             out_ref[1, place, :rows, :] = merge_right(sig, cot)
-            top, bottom = fil_ref[:quarter, lanes], fil_ref[quarter:, lanes]
-            out_ref[0, place, rows:, :] = merge(top, bottom)
-            out_ref[1, place, rows:, :] = merge_right(top, bottom)
 
 
 def unpack_kernel(in_ref, sig_hbm, fil_hbm, sig_ref, fil_ref, sent):

time: 78.5 us -> 78.5 us (level)
  no operation moved by 1% of the time
where the time goes in v9:
time: 78.5 us; the launch traced here: 78.3 us
  blocking collectives  69.3 us (88%)
  Pallas kernels  8.31 us (11%)
    all_to_all x2, blocking collectives, exchange(): lax.all_to_all(message, both, split_axis=0, concat_axis=0, tiled=True)  69.3 us
    pallas_call x1, Pallas kernels, core(): pl.pallas_call(kernel, in_specs=[vmem, vmem, vmem], out_specs=vmem, out_s...  5.43 us
    pallas_call x1, Pallas kernels, packed_body(): pl.pallas_call(pack_kernel, in_specs=[pl.BlockSpec(memory_space=pltpu.SME...  1.72 us

profile of v9, /device:TPU:0, one launch (start us, length us, event | category | flops | bytes accessed | tf_op | source)
XLA Modules:
  0.0 78.3 jit_solution(14264053996934741972)
XLA Ops:
  0.6 0.0 copy-start
  0.6 1.7 %pack.1 = bf16[2,16,160,128]{3,2,1,0:T(8,128)(2,1)S(1)} custom-call(s32[1]{0:T(128)} %bitcast.part_ref, bf16[128,2048]{1,0:T(8,128)(2,1)} %sig_hbm.1, bf16[128,2048]{1,0:T(8,128)(2,1)} %cot_hbm.1, bf16[128,2048]{1,0:T(8,128)(2,1)} %fil_hbm.1), custom_call_target="tpu_custom_call" | custom-call | tf_op jit(solution)/shard_map/pack/pallas_call | solution.py:311
  2.4 0.0 copy-start.1
  2.4 39.9 %all_to_all.10 = bf16[32,160,128]{2,1,0:T(8,128)(2,1)S(1)} all-to-all(bf16[32,160,128]{2,1,0:T(8,128)(2,1)S(1)} %bitcast.5), channel_id=1, replica_groups=mesh['tp'=2,'cp'=16] {'tp','cp'}, dimensions={0} | all-to-all | bytes 2621440 | tf_op jit(solution)/shard_map/all_to_all | solution.py:303
  42.3 0.0 copy-done
  42.3 0.0 copy-done.1
  42.3 5.4 %gradients.1 = bf16[2,16,128,128]{3,2,1,0:T(8,128)(2,1)S(1)} custom-call(bf16[16,256,256]{2,1,0:T(8,128)(2,1)S(1)} %copy-done.1, bf16[16,128,512]{2,1,0:T(8,128)(2,1)S(1)} %copy-done, bf16[2,16,160,128]{3,2,1,0:T(8,128)(2,1)S(1)} %bitcast.6), custom_call_target="tpu_custom_call" | custom-call | tf_op jit(solution)/shard_map/gradients/pallas_call | solution.py:289
  47.7 29.4 %all_to_all.11 = bf16[32,128,128]{2,1,0:T(8,128)(2,1)S(1)} all-to-all(bf16[32,128,128]{2,1,0:T(8,128)(2,1)S(1)} %bitcast.7), channel_id=1, replica_groups=mesh['tp'=2,'cp'=16] {'tp','cp'}, dimensions={0} | all-to-all | bytes 2097152 | tf_op jit(solution)/shard_map/all_to_all | solution.py:303
  77.2 1.2 %unpack.1 = (bf16[128,2048]{1,0:T(8,128)(2,1)}, bf16[128,2048]{1,0:T(8,128)(2,1)}) custom-call(bf16[2,16,128,128]{3,2,1,0:T(8,128)(2,1)S(1)} %bitcast.8), custom_call_target="tpu_custom_call" | custom-call | tf_op jit(solution)/shard_map/unpack/pallas_call | solution.py:327
Async XLA Ops:
  0.6 41.7 %copy-start = (bf16[16,128,512]{2,1,0:T(8,128)(2,1)S(1)}, bf16[16,128,512]{2,1,0:T(8,128)(2,1)}, u32[]{:S(2)}) copy-start(bf16[16,128,512]{2,1,0:T(8,128)(2,1)} %constant.11.clone.inverse_ref) | copy-start | bytes 6291460
  2.4 39.9 %copy-start.1 = (bf16[16,256,256]{2,1,0:T(8,128)(2,1)S(1)}, bf16[16,256,256]{2,1,0:T(8,128)(2,1)}, u32[]{:S(2)}) copy-start(bf16[16,256,256]{2,1,0:T(8,128)(2,1)} %constant.10.clone.forward_ref) | copy-start | bytes 6291460
